TPU v7x, 128 devices: a whole 4x4x4 slice. The times are simulated.
128 devices in a mesh: row: 8 (over x_lo, z), col: 16 (over y, x_hi, core).
Axes of the slice: x: 4 (x_hi: 2, x_lo: 2; x = x_hi * 2 + x_lo), y: 4, z: 4, core: 2. Of those that a mesh axis runs over, the one named last changes fastest.
Arguments:
- pool: bfloat16 [24576, 128], P(('row', 'col')), may hold values from -20 to 20
- labeled: bfloat16 [24576, 128], P(('row', 'col')), may hold values from -20 to 20
Outputs:
- grad_pool: float32 [24576, 128], P(('row', 'col'))
- grad_label: float32 [24576, 128], P(('row', 'col'))
- objective: float32 [], replicated
All inputs are finite; a program needn't handle non-finite values.
Results may differ from a plain program's by a relative error of at most 0.03.
Values may be sent and summed in bfloat16 or wider, within the bound.
A program may use at most 64 MiB of HBM per device.

v0:
```python
import jax
import jax.numpy as jnp
from jax import lax
from jax.sharding import PartitionSpec as P


def squared_norms(values):
    return jnp.sum(jnp.square(values.astype(jnp.float32)), axis=1)


def gram_kernel(left_rows, left_norms, right_rows, right_norms):
    products = lax.dot_general(
        left_rows, right_rows, (((1,), (1,)), ((), ())), preferred_element_type=jnp.float32
    )
    distance = left_norms[:, None] + right_norms[None, :] - 2.0 * products
    return jnp.exp(distance * (-0.5 / left_rows.shape[1]))


def shards(pool, labeled):
    width = pool.shape[1]
    own_rows = pool.shape[0]
    pool_rows, label_rows = (
        lax.all_gather(pool, "col", axis=0, tiled=True),
        lax.all_gather(labeled, "col", axis=0, tiled=True),
    )
    pool_cols, label_cols = (
        lax.all_gather(pool, "row", axis=0, tiled=True),
        lax.all_gather(labeled, "row", axis=0, tiled=True),
    )
    row_count = pool_rows.shape[0]
    col_count = pool_cols.shape[0]
    count = float(own_rows * lax.axis_size("row") * lax.axis_size("col"))
    block_rows = 512
    block_count = row_count // block_rows
    pool_cnorms = squared_norms(pool_cols)
    label_cnorms = squared_norms(label_cols)
    pool_blocks = pool_rows.reshape(block_count, block_rows, width)
    label_blocks = label_rows.reshape(block_count, block_rows, width)
    pool_nblocks = squared_norms(pool_rows).reshape(block_count, block_rows)
    label_nblocks = squared_norms(label_rows).reshape(block_count, block_rows)
    row_pieces = (pool_blocks, label_blocks, pool_nblocks, label_nblocks)

    def first_pass(column_sums, pieces):
        pool_part, label_part, pool_npart, label_npart = pieces
        kernel_xx = gram_kernel(pool_part, pool_npart, pool_cols, pool_cnorms)
        kernel_yy = gram_kernel(label_part, label_npart, label_cols, label_cnorms)
        kernel_xy = gram_kernel(pool_part, pool_npart, label_cols, label_cnorms)
        row_part = jnp.sum(kernel_xx + kernel_yy - kernel_xy, axis=1)
        return (column_sums + jnp.sum(kernel_xy, axis=0), row_part)

    column_sums, row_parts = lax.scan(first_pass, jnp.zeros((col_count,), jnp.float32), row_pieces)
    cross_totals = lax.psum_scatter(column_sums, "row", scatter_dimension=0, tiled=True)
    partial_rows = row_parts.reshape(row_count)
    first_sums = lax.psum_scatter(partial_rows, "col", scatter_dimension=0, tiled=True)
    own_totals = first_sums - cross_totals
    grand = lax.psum(jnp.sum(own_totals), ("row", "col"))
    mean_row = grand / count
    spread_sum = lax.psum(jnp.sum(jnp.square(own_totals - mean_row)), ("row", "col"))
    variance = 4.0 * spread_sum / count**3 + 1e-08
    statistic = mean_row / count
    objective = statistic / jnp.sqrt(variance)
    coef_a = 1.0 / (count * jnp.sqrt(variance))
    coef_b = -4.0 * statistic / (count**2 * variance**1.5)
    centred = own_totals - mean_row
    row_centred = lax.all_gather(centred, "col", axis=0, tiled=True)
    col_centred = lax.all_gather(centred, "row", axis=0, tiled=True)
    centre_blocks = row_centred.reshape(block_count, block_rows)
    second_pieces = (pool_blocks, label_blocks, pool_nblocks, label_nblocks, centre_blocks)

    def row_side(pieces):
        pool_part, label_part, pool_npart, label_npart, centre_part = pieces
        pair_weight = 2.0 * coef_a + coef_b * (centre_part[:, None] + col_centred[None, :])
        weight_xx = pair_weight * gram_kernel(pool_part, pool_npart, pool_cols, pool_cnorms)
        weight_yy = pair_weight * gram_kernel(label_part, label_npart, label_cols, label_cnorms)
        weight_xy = pair_weight * gram_kernel(pool_part, pool_npart, label_cols, label_cnorms)
        xy_rounded = weight_xy.astype(jnp.bfloat16)
        pool_grad = pool_part.astype(jnp.float32) * jnp.sum(weight_xx - weight_xy, axis=1)[:, None]
        pool_grad = pool_grad - jnp.dot(
            weight_xx.astype(jnp.bfloat16), pool_cols, preferred_element_type=jnp.float32
        )
        pool_grad = pool_grad + jnp.dot(xy_rounded, label_cols, preferred_element_type=jnp.float32)
        label_grad = label_part.astype(jnp.float32) * jnp.sum(weight_yy, axis=1)[:, None]
        label_grad = label_grad - jnp.dot(
            weight_yy.astype(jnp.bfloat16), label_cols, preferred_element_type=jnp.float32
        )
        return (pair_weight, weight_xy, xy_rounded, pool_grad, label_grad)

    def second_pass(label_column, pieces):
        pair_weight, weight_xy, xy_rounded, pool_grad, label_grad = row_side(pieces)
        cross = label_cols.astype(jnp.float32) * jnp.sum(weight_xy, axis=0)[:, None]
        cross = cross - lax.dot_general(
            xy_rounded, pieces[0], (((0,), (0,)), ((), ())), preferred_element_type=jnp.float32
        )
        return (label_column + cross, (pool_grad, label_grad))

    label_column, grads = lax.scan(
        second_pass, jnp.zeros((col_count, width), jnp.float32), second_pieces
    )
    label_extra = lax.psum_scatter(label_column, "row", scatter_dimension=0, tiled=True)
    pool_flat = grads[0].reshape(row_count, width)
    label_flat = grads[1].reshape(row_count, width)
    pool_own, label_own = (
        lax.psum_scatter(pool_flat, "col", scatter_dimension=0, tiled=True),
        lax.psum_scatter(label_flat, "col", scatter_dimension=0, tiled=True),
    )
    grad_pool = -pool_own / width
    grad_label = (label_extra - label_own) / width
    return (grad_pool, grad_label, objective)


def solution(mesh):
    in_specs = (P(("row", "col"), None), P(("row", "col"), None))
    out_specs = (P(("row", "col"), None), P(("row", "col"), None), P())
    return jax.shard_map(shards, mesh=mesh, in_specs=in_specs, out_specs=out_specs, check_vma=False)
```

profile of v0, /device:TPU:1, one launch (start us, length us, event | category | flops | bytes accessed | tf_op | source)
XLA Modules:
  0.0 678.3 jit_solution(6864748292042515302)
XLA Ops:
  7.2 25.1 %all_gather.20 = bf16[1536,128]{1,0:T(8,128)(2,1)S(1)} all-gather(bf16[192,128]{1,0:T(8,128)(2,1)} %param.6), channel_id=1, replica_groups=mesh['row'=8,'col'=16] {'row'}, dimensions={0}, use_global_device_ids=true | all-gather | bytes 442368 | tf_op jit(solution)/shard_map/all_gather | solution.py:27
  32.3 34.5 %all_gather.19 = bf16[3072,128]{1,0:T(8,128)(2,1)S(1)} all-gather(bf16[192,128]{1,0:T(8,128)(2,1)} %param.6), channel_id=1, replica_groups=mesh['row'=8,'col'=16] {'col'}, dimensions={0}, use_global_device_ids=true | all-gather | bytes 835584 | tf_op jit(solution)/shard_map/all_gather | solution.py:23
  66.8 22.9 %all_gather.18 = bf16[1536,128]{1,0:T(8,128)(2,1)S(1)} all-gather(bf16[192,128]{1,0:T(8,128)(2,1)} %param.7), channel_id=1, replica_groups=mesh['row'=8,'col'=16] {'row'}, dimensions={0}, use_global_device_ids=true | all-gather | bytes 442368 | tf_op jit(solution)/shard_map/all_gather | solution.py:28
  89.7 30.1 %all_gather.21 = bf16[3072,128]{1,0:T(8,128)(2,1)S(1)} all-gather(bf16[192,128]{1,0:T(8,128)(2,1)} %param.7), channel_id=1, replica_groups=mesh['row'=8,'col'=16] {'col'}, dimensions={0}, use_global_device_ids=true | all-gather | bytes 835584 | tf_op jit(solution)/shard_map/all_gather | solution.py:24
  125.2 19.2 %while.30 = (s32[]{:T(128)}, f32[1536]{0:T(1024)S(1)}, f32[6,512]{1,0:T(8,128)S(1)}, f32[6,512]{1,0:T(8,128)S(1)}, f32[1536]{0:T(1024)S(1)}, /*index=5*/bf16[6,5...) while((s32[]{:T(128)}, f32[1536]{0:T(1024)S(1)}, ...), condition=%wide.region_7.8_spmd.clone, body=%wide.region_4.7_spmd.clone.sunk | while | flops 616563712 | bytes 14225571 | solution.py:51
  144.4 61.1 %all-reduce.2 = f32[3072]{0:T(1024)S(1)} all-reduce(f32[3072]{0:T(1024)S(1)} %reshape.52), channel_id=2, replica_groups=mesh['row'=8,'col'=16] {'col'}, use_global_device_ids=true, to_apply=%region_8.9.clone | all-reduce | flops 3072 | bytes 24576
  205.5 15.7 %all-reduce.3 = f32[1536]{0:T(1024)S(1)} all-reduce(f32[1536]{0:T(1024)S(1)} %get-tuple-element.246), channel_id=3, replica_groups=mesh['row'=8,'col'=16] {'row'}, use_global_device_ids=true, to_apply=%region_9.10.clone | all-reduce | flops 1536 | bytes 12288
  221.9 71.1 %psum.14 = f32[]{:T(128)} all-reduce(f32[]{:T(128)} %get-tuple-element.393), channel_id=1, replica_groups=mesh['row'=8,'col'=16] {'row','col'}, use_global_device_ids=true, to_apply=%region_11.12 | all-reduce | flops 1 | bytes 8 | tf_op jit(solution)/shard_map/psum | solution.py:56
  295.1 63.0 %psum.15 = f32[]{:T(128)} all-reduce(f32[]{:T(128)} %get-tuple-element.405), channel_id=1, replica_groups=mesh['row'=8,'col'=16] {'row','col'}, use_global_device_ids=true, to_apply=%region_13.14 | all-reduce | flops 1 | bytes 8 | tf_op jit(solution)/shard_map/psum | solution.py:58
  358.9 13.9 %all-reduce.1 = f32[1536]{0:T(1024)S(1)} all-reduce(f32[1536]{0:T(1024)S(1)} %get-tuple-element.404), channel_id=1, replica_groups=mesh['row'=8,'col'=16] {'row'}, use_global_device_ids=true, to_apply=%add.1 | all-reduce | flops 1536 | bytes 12288
  372.8 63.6 %all-reduce = f32[3072]{0:T(1024)S(1)} all-reduce(f32[3072]{0:T(1024)S(1)} %get-tuple-element.406), channel_id=1, replica_groups=mesh['row'=8,'col'=16] {'col'}, use_global_device_ids=true, to_apply=%add | all-reduce | flops 3072 | bytes 24576
  436.5 53.3 %while.31 = (s32[]{:T(128)}, f32[1536,128]{1,0:T(8,128)S(1)}, f32[6,512,128]{2,1,0:T(8,128)}, f32[6,512,128]{2,1,0:T(8,128)}, bf16[1536,128]{1,0:T(8,128)(2,1)S(...) while((s32[]{:T(128)}, f32[1536,128]{1,0:T(8,128)S(1)}, ...), condition=%wide.region_18.19_spmd.clone, body=%wide.region_14.18_spmd.clone.sunk | while | flops 1435891200 | bytes 25131248 | solution.py:96
  441.0 2.1 subtract_reduce_fusion.2
  449.9 2.1 subtract_reduce_fusion.2
  454.3 1.4 fusion.140
  458.8 2.1 subtract_reduce_fusion.2
  467.7 2.1 subtract_reduce_fusion.2
  476.5 2.1 subtract_reduce_fusion.2
  485.4 2.1 subtract_reduce_fusion.2
  492.2 65.3 %reduce-scatter.4.cloned.1.call-done = f32[192,128]{1,0:T(8,128)} async-done(((f32[3072,128]{1,0:T(8,128)}), f32[192,128]{1,0:T(8,128)}) %reduce-scatter.4.cloned.1.call-update) | async-done | bytes 98320 | tf_op jit(solution)/shard_map/reduce_scatter | solution.py:103
  557.5 1.5 negate_multiply_fusion
  559.0 35.2 %reduce-scatter.6.cloned.1.call-done = f32[192,128]{1,0:T(8,128)} async-done(((f32[1536,128]{1,0:T(8,128)}), f32[192,128]{1,0:T(8,128)}) %reduce-scatter.6.cloned.1.call-update) | async-done | bytes 98320 | tf_op jit(solution)/shard_map/reduce_scatter | solution.py:99
  594.3 74.8 %reduce-scatter.8.cloned.1.call-done = f32[192,128]{1,0:T(8,128)} async-done(((f32[3072,128]{1,0:T(8,128)}), f32[192,128]{1,0:T(8,128)}) %reduce-scatter.8.cloned.1.call-update) | async-done | bytes 98320 | tf_op jit(solution)/shard_map/reduce_scatter | solution.py:104
  669.0 1.6 subtract_multiply_fusion
  (109 shorter events, 64.1 us)
Async XLA Ops:
  7.2 550.3 %reduce-scatter.4.cloned.1.call-start = ((), (), s32[]{:S(2)}) async-start(), calls=%async_computation.3 | async-start | bytes 1671168 | tf_op jit(solution)/shard_map/reduce_scatter | solution.py:103
  489.8 0.9 copy-start
  489.9 104.4 %reduce-scatter.6.cloned.1.call-start = ((), (), s32[]{:S(2)}) async-start(), calls=%async_computation.4 | async-start | bytes 884736 | tf_op jit(solution)/shard_map/reduce_scatter | solution.py:99
  490.7 178.3 %reduce-scatter.8.cloned.1.call-start = ((), (), s32[]{:S(2)}) async-start(), calls=%async_computation.5 | async-start | bytes 1671168 | tf_op jit(solution)/shard_map/reduce_scatter | solution.py:104
Sparse Core Ops, SparseCore 0:
  490.0 67.4 reduce-scatter.3
  560.0 34.2 reduce-scatter.5
  598.2 70.7 reduce-scatter.7
where the time goes:
time: 680 us; the launch traced here: 678 us
  blocking collectives  401 us (59%)
  waiting for transfers between devices  176 us (26%)
  matrix products  71.5 us (11%)
  between operations  20.3 us (3%)
    unnamed x4, blocking collectives  154 us
    reduce_scatter x1, waiting for transfers between devices, shards(): lax.psum_scatter(label_flat, 'col', scatter_dimension=0, tiled=True)  74.8 us
    psum x1, blocking collectives, shards(): grand = lax.psum(jnp.sum(own_totals), ('row', 'col'))  71.1 us
    reduce_scatter x1, waiting for transfers between devices, shards(): lax.psum_scatter(pool_flat, 'col', scatter_dimension=0, tiled=True)  65.3 us
    psum x1, blocking collectives, shards(): lax.psum(jnp.sum(jnp.square(own_totals - mean_row)), ('row', 'col'))  63 us
    dot_general x36, matrix products, gram_kernel(): lax.dot_general(left_rows, right_rows, (((1,), (1,)), ((), ())), preferre...  46.5 us
    reduce_scatter x1, waiting for transfers between devices, shards(): lax.psum_scatter(label_column, 'row', scatter_dimension=0, tiled=True)  35.2 us
    all_gather x1, blocking collectives, shards(): lax.all_gather(pool, 'col', axis=0, tiled=True)  34.5 us
  transfers between devices with their start and end apart: 3, of which 3 were waited for; matrix products, arithmetic and copies ran while one was open for 0% of the time, Pallas kernels for 0%

commit v1 on v0

v1 whole, which is shorter than its diff:
```python
import math

import jax
import jax.numpy as jnp
from jax import lax
from jax.experimental import pallas as pl
from jax.experimental.pallas import tpu as pltpu
from jax.sharding import PartitionSpec as P

MESH = pl.DeviceIdType.MESH
F32 = jnp.float32
BF16 = jnp.bfloat16

FIRST = tuple((dx, dk) for dx in range(4) for dk in range(2))
SECOND = ((0, 1), (1, 0), (-1, -1), (-1, 1), (1, 2), (2, -1), (0, 0), (0, 2), (2, 0), (2, 2))
OWN_FIRST = FIRST.index((0, 0))
OWN_SECOND = SECOND.index((0, 0))
TWO_SIDED = 3
SECOND_PAIRS = len(SECOND) // 2


def place():
    row, col = lax.axis_index("row"), lax.axis_index("col")
    return ((col // 2) % 2) * 2 + row // 4, col // 4, row % 4, col % 2


def device(x, y, z, core):
    x, y, z, core = (x + 8) % 4, (y + 8) % 4, (z + 8) % 4, (core + 2) % 2
    return ((x % 2) * 4 + z, y * 4 + (x // 2) * 2 + core)


def split3(value):
    high = value.astype(BF16).astype(F32)
    rest = value - high
    middle = rest.astype(BF16).astype(F32)
    return high, middle, rest - middle


def matmul(left, right):
    return lax.dot_general(left, right, (((1,), (0,)), ((), ())), preferred_element_type=F32)


def matmul_t(left, right):
    return lax.dot_general(left, right, (((1,), (1,)), ((), ())), preferred_element_type=F32)


def kernel(
    pool_ref, label_ref, grad_pool_ref, grad_label_ref, objective_ref,
    own, at, bt, za, km, acc_a, acc_b, part_a, part_b, part_in, t_own, ta, tb,
    w1a, w1b, w2a, w2b, o1a, o1b, o2a, o2b, ga, gb, g_in, stat_out, stat_in,
    ga_send, ga_recv, gb_send, gb_recv, pa_send, pa_recv, pb_send, pb_recv,
    ta_send, ta_recv, tb_send, tb_recv, ra_send, ra_recv, rb_send, rb_recv, st_send, st_recv,
):
    width = pool_ref.shape[1]
    each = pool_ref.shape[0]
    both = 2 * each
    deep = width + 16
    na, nb = len(FIRST), len(SECOND)
    points = float(each * 128)
    x, y, z, core = place()

    def to_first(a):
        dx, dk = FIRST[a]
        return device(x + dx, y, z, core + dk)

    def from_first(a):
        dx, dk = FIRST[a]
        return device(x - dx, y, z, core + dk)

    def to_second(b):
        dy, dz = SECOND[b]
        return device(x, y + dy, z + dz, core)

    def from_second(b):
        dy, dz = SECOND[b]
        return device(x, y - dy, z - dz, core)

    def copy(src, dst, send, recv, target):
        return pltpu.make_async_remote_copy(
            src_ref=src, dst_ref=dst, send_sem=send, recv_sem=recv, device_id=target, device_id_type=MESH
        )

    first_others = [a for a in range(na) if a != OWN_FIRST]
    second_others = [b for b in range(nb) if b != OWN_SECOND]

    def lanes(index, count=1):
        return pl.ds(pl.multiple_of(index * both * count, both * count), both * count)

    partners = set()
    for a in first_others:
        dx, dk = FIRST[a]
        partners.add((dx, 0, 0, dk))
    for b in second_others:
        dy, dz = SECOND[b]
        partners.add((0, dy % 4, dz % 4, 0))
        partners.add((0, -dy % 4, -dz % 4, 0))
    barrier = pltpu.get_barrier_semaphore()
    for dx, dy, dz, dk in sorted(partners):
        pl.semaphore_signal(
            barrier, inc=1, device_id=device(x + dx, y + dy, z + dz, core + dk), device_id_type=MESH
        )

    sign = jnp.where(lax.broadcasted_iota(jnp.int32, (1, both), 1) < each, 1.0, -1.0).astype(F32)
    rows = jnp.concatenate([pool_ref[...].astype(F32), label_ref[...].astype(F32)], axis=0)
    cols = rows.T
    half = jnp.sum(cols * cols, axis=0, keepdims=True) * -0.5
    high, middle, low = split3(half)
    place16 = lax.broadcasted_iota(jnp.int32, (16, both), 0)
    tail = jnp.where(place16 == 0, high, jnp.where(place16 == 1, middle, jnp.where(place16 == 2, low, 0.0)))
    tail = jnp.where((place16 >= 8) & (place16 < 11), 1.0, tail)
    block = jnp.concatenate([cols, tail], axis=0).astype(BF16)
    own[...] = block
    at[:, pl.ds(OWN_FIRST * both, both)] = block
    bt[0:deep, pl.ds(OWN_SECOND * both, both)] = block
    bt[deep:, :] = jnp.zeros((bt.shape[0] - deep, nb * both), BF16)
    acc_a[...] = jnp.zeros(acc_a.shape, F32)
    acc_b[...] = jnp.zeros(acc_b.shape, F32)

    pl.semaphore_wait(barrier, len(partners))

    gathers = []
    for a in first_others[:1]:
        gathers.append(copy(own, at.at[:, pl.ds(a * both, both)], ga_send.at[a], ga_recv.at[a], from_first(a)))
    for b in second_others:
        gathers.append(
            copy(own, bt.at[pl.ds(0, deep), pl.ds(b * both, both)], gb_send.at[b], gb_recv.at[b], from_second(b))
        )
    for a in first_others[1:]:
        gathers.append(copy(own, at.at[:, pl.ds(a * both, both)], ga_send.at[a], ga_recv.at[a], from_first(a)))
    for item in gathers:
        item.start()

    one_row = jnp.where(lax.broadcasted_iota(jnp.int32, (16, both), 0) == 0, sign, 0.0)

    def take_first(a):
        here = lanes(a)
        value = at[:, here].astype(F32)
        za[here, 0:width] = value[0:width].T.astype(BF16)
        rest = jnp.concatenate(
            [value[width + 8 : width + 16], value[width : width + 8], jnp.zeros((width - 16, both), F32)], axis=0
        )
        za[here, width : 2 * width] = rest.T.astype(BF16)
        w1a[0:width, here] = (value[0:width] * sign).astype(BF16)
        w1a[width:deep, here] = one_row.astype(BF16)

    def take_second(b):
        here = lanes(b)
        value = bt[0:width, here].astype(F32)
        w1b[0:width, here] = (value * sign).astype(BF16)
        w1b[width:deep, here] = one_row.astype(BF16)

    scale = math.log2(math.e) / width
    tile_sign = sign[:, 128:256]

    def second_step(i, carry):
        pair = i + jnp.where(i == 2, 1, 0) - jnp.where(i == 3, 1, 0)

        def await_second(b):
            @pl.when(b != OWN_SECOND)
            def _():
                copy(
                    own, bt.at[pl.ds(0, deep), lanes(b)], gb_send.at[b], gb_recv.at[b], device(x, y, z, core)
                ).wait_recv()

            take_second(b)

        await_second(2 * pair)
        await_second(2 * pair + 1)
        wide = lanes(pair, 2)

        def first_step(a, carry):
            here = lanes(a)

            @pl.when((i == 0) & (a != OWN_FIRST))
            def _():
                copy(own, at.at[:, here], ga_send.at[a], ga_recv.at[a], device(x, y, z, core)).wait_recv()

            @pl.when(i == 0)
            def _():
                take_first(a)

            product = matmul(za[here, :], bt[:, wide])
            value = jnp.exp2(product * scale)
            km[here, wide] = value.astype(BF16)
            tiles = [value[:, 128 * j : 128 * (j + 1)] for j in range(6)]
            across = (tiles[0] - tiles[2]) + (tiles[3] - tiles[5]) + (tiles[1] + tiles[4]) * tile_sign
            acc_a[here, :] += across
            down = jnp.sum(value[0:each].reshape(each // 8, 8, 2 * both), axis=0)
            down = down - jnp.sum(value[each:both].reshape(each // 8, 8, 2 * both), axis=0)
            unused = (pair >= TWO_SIDED) & ((a < 2) | (a >= 4))
            to = pl.multiple_of(jnp.where(unused, 8, 0), 8)
            acc_b[pl.ds(to, 8), wide] += down
            return carry

        lax.fori_loop(0, jnp.where(pair < TWO_SIDED, na, 6), first_step, 0)
        return carry

    lax.fori_loop(0, SECOND_PAIRS, second_step, 0)

    for b in range(nb):
        here = pl.ds(b * both, both)
        part_b[:, here] = jnp.broadcast_to(jnp.sum(acc_b[0:8, here], axis=0, keepdims=True) * sign, (8, both))
    partials = []
    for b in second_others:
        here = pl.ds(b * both, both)
        partials.append(copy(part_b.at[:, here], part_in.at[na + b], pb_send.at[b], pb_recv.at[b], to_second(b)))
        partials[-1].start()
    for a in list(reversed(first_others)) + [OWN_FIRST]:
        here = pl.ds(a * both, both)
        total = jnp.sum(acc_a[here, :].T, axis=0, keepdims=True) * sign
        part_a[:, here] = jnp.broadcast_to(total, (8, both))
        if a != OWN_FIRST:
            partials.append(copy(part_a.at[:, here], part_in.at[a], pa_send.at[a], pa_recv.at[a], to_first(a)))
            partials[-1].start()

    inner = TWO_SIDED * 2 * both

    def sum_first(w, out, w_cols, ap):
        here = lanes(ap, 2)
        out[:, here] = matmul_t(w[:, 0:w_cols], km[here, 0:w_cols])

    def sum_second(w, out, bp, lo, hi):
        here = lanes(bp, 2)
        out[:, here] = matmul(w[:, lo:hi], km[lo:hi, here])

    def all_sums(wa, wb, oa, ob):
        def body_b(bp, carry):
            sum_second(wa, ob, bp, 0, na * both)
            return carry

        def body_b2(bp, carry):
            sum_second(wa, ob, bp, 2 * both, 4 * both)
            return carry

        def body_a(ap, carry):
            sum_first(wb, oa, nb * both, ap)
            return carry

        lax.fori_loop(0, TWO_SIDED, body_b, 0)
        lax.fori_loop(TWO_SIDED, SECOND_PAIRS, body_b2, 0)
        lax.fori_loop(0, 3, body_a, 0)
        sum_first(wb, oa, inner, 3)

    all_sums(w1a, w1b, o1a, o1b)

    for item in partials:
        item.wait_recv()
    total = part_a[:, pl.ds(OWN_FIRST * both, both)] + part_b[:, pl.ds(OWN_SECOND * both, both)]
    for a in first_others:
        total = total + part_in[a]
    for b in second_others:
        total = total + part_in[na + b]
    total = total + pltpu.roll(total, each, 1)
    t_own[...] = total
    ta[:, pl.ds(OWN_FIRST * both, both)] = total
    tb[:, pl.ds(OWN_SECOND * both, both)] = total
    totals = []
    for a in first_others:
        totals.append(copy(t_own, ta.at[:, pl.ds(a * both, both)], ta_send.at[a], ta_recv.at[a], from_first(a)))
    for b in second_others:
        totals.append(copy(t_own, tb.at[:, pl.ds(b * both, both)], tb_send.at[b], tb_recv.at[b], from_second(b)))
    for item in totals:
        item.start()
    for item in totals[: len(first_others)]:
        item.wait_recv()

    line = ta[0:1, :]
    mean = jnp.sum(line, axis=1, keepdims=True) / (na * both)
    spread = 0.5 * jnp.sum(jnp.square(line - mean), axis=1, keepdims=True)

    def send_stats(stage, mean, spread):
        half_lane = lax.broadcasted_iota(jnp.int32, (8, 128), 1) < 64
        stat_out[stage] = jnp.where(half_lane, mean, spread)
        items = []
        for step in range(1, 4):
            target = device(x, y - step, z, core) if stage == 0 else device(x, y, z - step, core)
            slot = stage * 3 + step - 1
            items.append(copy(stat_out.at[stage], stat_in.at[slot], st_send.at[slot], st_recv.at[slot], target))
            items[-1].start()
        return items

    def merge_stats(stage, items, mean, spread, count):
        means, spreads = [mean], [spread]
        for item in items:
            item.wait_recv()
        for step in range(3):
            value = stat_in[stage * 3 + step]
            means.append(value[0:1, 0:1])
            spreads.append(value[0:1, 64:65])
        middle = (means[0] + means[1] + means[2] + means[3]) * 0.25
        total = spreads[0] + spreads[1] + spreads[2] + spreads[3]
        for value in means:
            total = total + count * jnp.square(value - middle)
        return middle, total

    stats_y = send_stats(0, mean, spread)
    for item in totals[len(first_others) :]:
        item.wait_recv()

    local = (jnp.sum(ta[0:1, :], axis=1, keepdims=True) + jnp.sum(tb[0:1, :], axis=1, keepdims=True)) / (
        (na + nb) * both
    )

    def weigh(t_ref, w1, w2, index):
        here = lanes(index)
        shifted = t_ref[0:1, here] - local
        w2[0:width, here] = (w1[0:width, here].astype(F32) * shifted).astype(BF16)
        high, middle, low = split3(shifted * sign)
        rows3 = jnp.where(place16 == 0, high, jnp.where(place16 == 1, middle, jnp.where(place16 == 2, low, 0.0)))
        w2[width:deep, here] = rows3.astype(BF16)

    def weigh_first(a, carry):
        weigh(ta, w1a, w2a, a)
        return carry

    def weigh_second(b, carry):
        weigh(tb, w1b, w2b, b)
        return carry

    lax.fori_loop(0, na, weigh_first, 0)
    lax.fori_loop(0, nb, weigh_second, 0)
    count8 = float(na * each)
    mean, spread = merge_stats(0, stats_y, mean, spread, count8)
    stats_z = send_stats(1, mean, spread)
    all_sums(w2a, w2b, o2a, o2b)
    mean, spread = merge_stats(1, stats_z, mean, spread, 4.0 * count8)

    variance = 4.0 * spread / points**3 + 1e-08
    statistic = mean / points
    deviation = jnp.sqrt(variance)
    coef_a = 1.0 / (points * deviation)
    coef_b = -4.0 * statistic / (points**2 * (variance * deviation))
    objective_ref[...] = jnp.broadcast_to(statistic / deviation, objective_ref.shape)
    base = 2.0 * coef_a + 2.0 * coef_b * (local - mean)

    def gradient(rows_ref, t_ref, o1, o2, index):
        here = pl.ds(index * both, both)
        value = rows_ref[0:width, here].astype(F32)
        plain = value * o1[width : width + 1, here] - o1[0:width, here]
        rho = o2[width : width + 1, here] + o2[width + 1 : width + 2, here] + o2[width + 2 : width + 3, here]
        weighted = value * rho - o2[0:width, here]
        alpha = base + coef_b * (t_ref[0:1, here] - local)
        outer = sign * (-1.0 / width)
        return plain * (alpha * outer) + weighted * (coef_b * outer)

    returns = []
    for b in reversed(second_others):
        here = pl.ds(b * both, both)
        gb[:, here] = gradient(bt, tb, o1b, o2b, b).astype(BF16)
        returns.append(copy(gb.at[:, here], g_in.at[na + b], rb_send.at[b], rb_recv.at[b], to_second(b)))
        returns[-1].start()
    for a in reversed(first_others):
        here = pl.ds(a * both, both)
        ga[:, here] = gradient(at, ta, o1a, o2a, a).astype(BF16)
        returns.append(copy(ga.at[:, here], g_in.at[a], ra_send.at[a], ra_recv.at[a], to_first(a)))
        returns[-1].start()
    result = gradient(at, ta, o1a, o2a, OWN_FIRST) + gradient(bt, tb, o1b, o2b, OWN_SECOND)
    for item in returns:
        item.wait_recv()
    for a in first_others:
        result = result + g_in[a].astype(F32)
    for b in second_others:
        result = result + g_in[na + b].astype(F32)
    result = result.T
    grad_pool_ref[...] = result[0:each]
    grad_label_ref[...] = result[each:both]

    for item in gathers + partials + totals + stats_y + stats_z + returns:
        item.wait_send()


def shards(pool, labeled):
    each, width = pool.shape
    both = 2 * each
    deep = width + 16
    na, nb = len(FIRST), len(SECOND)
    la, lb = na * both, nb * both
    dma = pltpu.SemaphoreType.DMA
    vmem = pl.BlockSpec(memory_space=pltpu.VMEM)
    scratch = [
        pltpu.VMEM((deep, both), BF16),
        pltpu.VMEM((deep, la), BF16),
        pltpu.VMEM((2 * width, lb), BF16),
        pltpu.VMEM((la, 2 * width), BF16),
        pltpu.VMEM((la, lb), BF16),
        pltpu.VMEM((la, 128), F32),
        pltpu.VMEM((16, lb), F32),
        pltpu.VMEM((8, la), F32),
        pltpu.VMEM((8, lb), F32),
        pltpu.VMEM((na + nb, 8, both), F32),
        pltpu.VMEM((8, both), F32),
        pltpu.VMEM((8, la), F32),
        pltpu.VMEM((8, lb), F32),
        pltpu.VMEM((deep, la), BF16),
        pltpu.VMEM((deep, lb), BF16),
        pltpu.VMEM((deep, la), BF16),
        pltpu.VMEM((deep, lb), BF16),
        pltpu.VMEM((deep, la), F32),
        pltpu.VMEM((deep, lb), F32),
        pltpu.VMEM((deep, la), F32),
        pltpu.VMEM((deep, lb), F32),
        pltpu.VMEM((width, la), BF16),
        pltpu.VMEM((width, lb), BF16),
        pltpu.VMEM((na + nb, width, both), BF16),
        pltpu.VMEM((2, 8, 128), F32),
        pltpu.VMEM((6, 8, 128), F32),
    ]
    for _ in range(4):
        scratch += [dma((na,)), dma((na,)), dma((nb,)), dma((nb,))]
    scratch += [dma((6,)), dma((6,))]
    grad_pool, grad_label, objective = pl.pallas_call(
        kernel,
        out_shape=(
            jax.ShapeDtypeStruct((each, width), F32),
            jax.ShapeDtypeStruct((each, width), F32),
            jax.ShapeDtypeStruct((8, 128), F32),
        ),
        in_specs=[vmem, vmem],
        out_specs=(vmem, vmem, vmem),
        scratch_shapes=scratch,
        compiler_params=pltpu.CompilerParams(
            collective_id=0, has_side_effects=True, vmem_limit_bytes=60 * 2**20
        ),
    )(pool, labeled)
    return grad_pool, grad_label, objective[0, 0]


def solution(mesh):
    in_specs = (P(("row", "col"), None), P(("row", "col"), None))
    out_specs = (P(("row", "col"), None), P(("row", "col"), None), P())
    return jax.shard_map(shards, mesh=mesh, in_specs=in_specs, out_specs=out_specs, check_vma=False)
```

time: 680 us -> 84 us (0.12)
  blocking collectives: 401 us -> 0 us
  waiting for transfers between devices: 176 us -> 0 us
  Pallas kernels: 0 us -> 79.7 us
  matrix products: 71.5 us -> 0 us
  between operations: 20.3 us -> 0.64 us
    reduce_scatter x3 -> x0, waiting for transfers between devices: 175 us -> none  [the longest x1 74.8 us: shards(): lax.psum_scatter(label_flat, 'col', scatter_dimension=0, tiled=True)]
    unnamed x4 -> x0, blocking collectives: 154 us -> none
    psum x2 -> x0, blocking collectives: 134 us -> none  [the longest x1 71.1 us: shards(): grand = lax.psum(jnp.sum(own_totals), ('row', 'col'))]
    all_gather x4 -> x0, blocking collectives: 112 us -> none  [the longest x1 34.5 us: shards(): lax.all_gather(pool, 'col', axis=0, tiled=True)]
    pallas_call x0 -> x1, Pallas kernels: none -> 79.7 us  [shards(): pl.pallas_call(kernel, out_shape=(jax.ShapeDtypeStruct((each, width), F32...]
    dot_general x60 -> x0, matrix products: 71.5 us -> none  [the longest x36 46.5 us: gram_kernel(): lax.dot_general(left_rows, right_rows, (((1,), (1,)), ((), ())), preferre...]
  transfers between devices with their start and end apart: 3 -> 0, of which waited for: 3 -> 0; matrix products, arithmetic and copies ran while one was open for 0% -> 0% of each run, Pallas kernels for 0% -> 0%
where the time goes in v1:
time: 84 us; the launch traced here: 83.7 us
  Pallas kernels  79.7 us (95%)
  local copies, waits for them, and re-layouts  3.4 us (4%)
    pallas_call x1, Pallas kernels, shards(): pl.pallas_call(kernel, out_shape=(jax.ShapeDtypeStruct((each, width), F32...  79.7 us
    unnamed x4, local copies, waits for them, and re-layouts  2.22 us

profile of v1, /device:TPU:1, one launch (start us, length us, event | category | flops | bytes accessed | tf_op | source)
XLA Modules:
  0.0 83.7 jit_solution(15224872224982855286)
XLA Ops:
  0.6 79.7 %shard_map.49 = (f32[192,128]{1,0:T(8,128)}, f32[192,128]{1,0:T(8,128)}, f32[8,128]{1,0:T(8,128)}) custom-call(bf16[192,128]{1,0:T(8,128)(2,1)} %pool_ref.1, bf16[192,128]{1,0:T(8,128)(2,1)} %label_ref.1), custom_call_target="tpu_custom_call" | custom-call | tf_op jit(solution)/shard_map/pallas_call | solution.py:411
  80.3 1.2 %slice.3 = f32[1,1]{1,0:T(1,128)} slice(f32[8,128]{1,0:T(8,128)} %get-tuple-element.8), slice={[0:1], [0:1]} | slice | bytes 8 | tf_op jit(solution)/shard_map/slice | solution.py:425
  81.5 0.0 copy-start
  81.5 1.6 %copy.7 = f32[192,128]{1,0:T(8,128)} copy(f32[192,128]{1,0:T(8,128)} %get-tuple-element.12) | data formatting | bytes 196608
  83.1 0.0 copy-done
  83.1 0.6 copy.8
Async XLA Ops:
  81.5 1.6 %copy-start = (f32[192,128]{1,0:T(8,128)S(1)}, f32[192,128]{1,0:T(8,128)}, u32[]{:S(2)}) copy-start(f32[192,128]{1,0:T(8,128)} %get-tuple-element.13) | copy-start | bytes 294916

commit v2 on v1

v2 whole, which is shorter than its diff:
```python
import math

import jax
import jax.numpy as jnp
from jax import lax
from jax.experimental import pallas as pl
from jax.experimental.pallas import tpu as pltpu
from jax.sharding import PartitionSpec as P

MESH = pl.DeviceIdType.MESH
F32 = jnp.float32
BF16 = jnp.bfloat16

FIRST = tuple((dx, dk) for dx in range(4) for dk in range(2))
SECOND = ((0, 1), (1, 0), (-1, -1), (-1, 1), (1, 2), (2, -1), (0, 0), (0, 2), (2, 0), (2, 2))
OWN_FIRST = FIRST.index((0, 0))
OWN_SECOND = SECOND.index((0, 0))
TWO_SIDED = 3
SECOND_PAIRS = len(SECOND) // 2


def place():
    row, col = lax.axis_index("row"), lax.axis_index("col")
    return ((col // 2) % 2) * 2 + row // 4, col // 4, row % 4, col % 2


def device(x, y, z, core):
    x, y, z, core = (x + 8) % 4, (y + 8) % 4, (z + 8) % 4, (core + 2) % 2
    return ((x % 2) * 4 + z, y * 4 + (x // 2) * 2 + core)


def split3(value):
    high = value.astype(BF16).astype(F32)
    rest = value - high
    middle = rest.astype(BF16).astype(F32)
    return high, middle, rest - middle


def matmul(left, right):
    return lax.dot_general(left, right, (((1,), (0,)), ((), ())), preferred_element_type=F32)


def matmul_t(left, right):
    return lax.dot_general(left, right, (((1,), (1,)), ((), ())), preferred_element_type=F32)


def pick(index, values):
    out = values[-1]
    for i in range(len(values) - 2, -1, -1):
        out = jnp.where(index == i, values[i], out)
    return out


def kernel(
    pool_ref, label_ref, grad_pool_ref, grad_label_ref, objective_ref,
    own, at, bt, za, km, acc_a, acc_b, part_a, part_b, part_in, t_own, ta, tb,
    w1a, w2a, wb, o1b, o2b, oa, ga, gb, g_in, stat_out, stat_in,
    ga_send, ga_recv, gb_send, gb_recv, pa_send, pa_recv, pb_send, pb_recv,
    ta_send, ta_recv, tb_send, tb_recv, ra_send, ra_recv, rb_send, rb_recv, st_send, st_recv,
):
    width = pool_ref.shape[1]
    each = pool_ref.shape[0]
    both = 2 * each
    deep = width + 16
    na, nb = len(FIRST), len(SECOND)
    points = float(each * 128)
    x, y, z, core = place()

    def to_first(a):
        return device(x + a // 2, y, z, core + a % 2)

    def from_first(a):
        return device(x - a // 2, y, z, core + a % 2)

    def to_second(b):
        return device(x, y + pick(b, [v[0] for v in SECOND]), z + pick(b, [v[1] for v in SECOND]), core)

    def from_second(b):
        return device(x, y - pick(b, [v[0] for v in SECOND]), z - pick(b, [v[1] for v in SECOND]), core)

    def copy(src, dst, send, recv, target):
        return pltpu.make_async_remote_copy(
            src_ref=src, dst_ref=dst, send_sem=send, recv_sem=recv, device_id=target, device_id_type=MESH
        )

    first_others = [a for a in range(na) if a != OWN_FIRST]
    second_others = [b for b in range(nb) if b != OWN_SECOND]

    def lanes(index, count=1):
        return pl.ds(pl.multiple_of(index * both * count, both * count), both * count)

    def block_lanes(index):
        return pl.ds(pl.multiple_of(index * both, both), both)

    def gather_first(a):
        return copy(own, at.at[:, block_lanes(a)], ga_send.at[a], ga_recv.at[a], from_first(a))

    def gather_second(b):
        return copy(
            own, bt.at[pl.ds(0, width), block_lanes(b)], gb_send.at[b], gb_recv.at[b], from_second(b)
        )

    def partial_first(a):
        return copy(part_a.at[:, block_lanes(a)], part_in.at[a], pa_send.at[a], pa_recv.at[a], to_first(a))

    def partial_second(b):
        return copy(part_b.at[:, block_lanes(b)], part_in.at[na + b], pb_send.at[b], pb_recv.at[b], to_second(b))

    def total_first(a):
        return copy(t_own, ta.at[:, block_lanes(a)], ta_send.at[a], ta_recv.at[a], from_first(a))

    def total_second(b):
        return copy(t_own, tb.at[:, block_lanes(b)], tb_send.at[b], tb_recv.at[b], from_second(b))

    def return_first(a):
        return copy(ga.at[:, block_lanes(a)], g_in.at[a], ra_send.at[a], ra_recv.at[a], to_first(a))

    def return_second(b):
        return copy(gb.at[:, block_lanes(b)], g_in.at[na + b], rb_send.at[b], rb_recv.at[b], to_second(b))

    def stats(slot):
        target = device(x, y - slot // 4, z - slot % 4, core)
        return copy(stat_out, stat_in.at[slot], st_send.at[slot], st_recv.at[slot], target)

    partners = [(dx, 0, 0, dk) for dx, dk in FIRST if (dx, dk) != (0, 0)]
    partners += [(0, slot // 4, slot % 4, 0) for slot in range(1, 16)]
    barrier = pltpu.get_barrier_semaphore()
    for dx, dy, dz, dk in partners:
        pl.semaphore_signal(
            barrier, inc=1, device_id=device(x + dx, y + dy, z + dz, core + dk), device_id_type=MESH
        )

    sign = jnp.where(lax.broadcasted_iota(jnp.int32, (1, both), 1) < each, 1.0, -1.0).astype(F32)
    rows = jnp.concatenate([pool_ref[...].astype(F32), label_ref[...].astype(F32)], axis=0)
    block = rows.T.astype(BF16)
    own[...] = block
    at[:, pl.ds(OWN_FIRST * both, both)] = block
    bt[0:width, pl.ds(OWN_SECOND * both, both)] = block
    bt[deep:, :] = jnp.zeros((bt.shape[0] - deep, nb * both), BF16)
    acc_a[...] = jnp.zeros(acc_a.shape, F32)
    acc_b[...] = jnp.zeros(acc_b.shape, F32)

    pl.semaphore_wait(barrier, len(partners))

    for b in (0, 1):
        gather_second(b).start()
    for a in (1, 2, 3):
        gather_first(a).start()
    for b in (2, 3):
        gather_second(b).start()
    for a in (6, 7):
        gather_first(a).start()
    for b in (7, 4, 5):
        gather_second(b).start()
    for a in (4, 5):
        gather_first(a).start()
    for b in (8, 9):
        gather_second(b).start()

    place8 = lax.broadcasted_iota(jnp.int32, (8, both), 0)
    none8 = jnp.zeros((8, both), F32)
    ones8 = jnp.where(place8 < 3, 1.0, none8)
    sign8 = jnp.where(place8 == 0, sign, none8)

    def three_rows(parts, start):
        out = none8
        for i, part in enumerate(parts):
            out = jnp.where(place8 == start + i, part, out)
        return out

    def half_norms(value):
        return three_rows(split3(jnp.sum(value * value, axis=0, keepdims=True) * -0.5), 0)

    def take_first(a):
        here = block_lanes(a)
        value = at[:, here].astype(F32)
        za[here, 0:width] = value.T.astype(BF16)
        rest = jnp.concatenate([ones8, half_norms(value), jnp.zeros((width - 16, both), F32)], axis=0)
        za[here, width : 2 * width] = rest.T.astype(BF16)
        w1a[0:width, here] = (value * sign).astype(BF16)
        w1a[width:deep, here] = jnp.concatenate([sign8, none8], axis=0).astype(BF16)

    def take_second(b):
        here = block_lanes(b)
        value = bt[0:width, here].astype(F32)
        bt[width:deep, here] = jnp.concatenate([half_norms(value), ones8], axis=0).astype(BF16)
        wb[0:width, here] = (value * sign).astype(BF16)

    scale = math.log2(math.e) / width
    tile_sign = sign[:, 128:256]

    def order(i):
        return i + jnp.where(i == 2, 1, 0) - jnp.where(i == 3, 1, 0)

    def sum_second(w, out, pair):
        here = lanes(pair, 2)

        @pl.when(pair < TWO_SIDED)
        def _():
            out[:, here] = matmul(w[...], km[:, here])

        @pl.when(pair >= TWO_SIDED)
        def _():
            out[:, here] = matmul(w[:, 2 * both : 4 * both], km[2 * both : 4 * both, here])

    def second_step(i, carry):
        pair = order(i)

        @pl.when(i > 0)
        def _():
            sum_second(w1a, o1b, order(i - 1))

        def await_second(b):
            @pl.when(b != OWN_SECOND)
            def _():
                gather_second(b).wait_recv()

            take_second(b)

        await_second(2 * pair)
        await_second(2 * pair + 1)
        wide = lanes(pair, 2)

        def first_step(ap, carry):
            @pl.when(i == 0)
            def _():
                @pl.when(ap > 0)
                def _():
                    gather_first(2 * ap).wait_recv()

                gather_first(2 * ap + 1).wait_recv()
                take_first(2 * ap)
                take_first(2 * ap + 1)

            here = lanes(ap, 2)
            product = matmul(za[here, :], bt[:, wide])
            value = jnp.exp2(product * scale)
            km[here, wide] = value.astype(BF16)
            tiles = [value[:, 128 * j : 128 * (j + 1)] for j in range(6)]
            across = (tiles[0] - tiles[2]) + (tiles[3] - tiles[5]) + (tiles[1] + tiles[4]) * tile_sign
            acc_a[here, :] += across
            parts = [
                jnp.sum(value[each * j : each * (j + 1)].reshape(each // 8, 8, 2 * both), axis=0) for j in range(4)
            ]
            unused = (pair >= TWO_SIDED) & (ap != 1)
            to = pl.multiple_of(jnp.where(unused, 8, 0), 8)
            acc_b[pl.ds(to, 8), wide] += (parts[0] - parts[1]) + (parts[2] - parts[3])
            return carry

        lax.fori_loop(0, jnp.where(pair < TWO_SIDED, 4, 3), first_step, 0)

        for b in (2 * pair, 2 * pair + 1):
            here = block_lanes(b)
            part_b[:, here] = jnp.broadcast_to(jnp.sum(acc_b[0:8, here], axis=0, keepdims=True) * sign, (8, both))

            @pl.when(b != OWN_SECOND)
            def _():
                partial_second(b).start()

        return carry

    lax.fori_loop(0, SECOND_PAIRS, second_step, 0)

    for a in (4, 5, 2, 3, 6, 7, 1, 0):
        here = pl.ds(a * both, both)
        total = jnp.sum(acc_a[here, :].T, axis=0, keepdims=True) * sign
        part_a[:, here] = jnp.broadcast_to(total, (8, both))
        if a != OWN_FIRST:
            partial_first(a).start()
    sum_second(w1a, o1b, SECOND_PAIRS - 1)

    total = part_a[:, pl.ds(OWN_FIRST * both, both)] + part_b[:, pl.ds(OWN_SECOND * both, both)]
    for b in second_others:
        partial_second(b).wait_recv()
        total = total + part_in[na + b]
    for a in first_others:
        partial_first(a).wait_recv()
        total = total + part_in[a]
    total = total + pltpu.roll(total, each, 1)
    t_own[...] = total
    ta[:, pl.ds(OWN_FIRST * both, both)] = total
    tb[:, pl.ds(OWN_SECOND * both, both)] = total
    for a in first_others:
        total_first(a).start()
    for b in second_others:
        total_second(b).start()
    for a in first_others:
        total_first(a).wait_recv()

    line = ta[0:1, :]
    local = jnp.sum(line, axis=1, keepdims=True) / (na * both)
    spread = 0.5 * jnp.sum(jnp.square(line - local), axis=1, keepdims=True)
    shared = jnp.where(lax.broadcasted_iota(jnp.int32, (8, 128), 1) < 64, local, spread)
    stat_out[...] = shared
    stat_in[0] = shared
    for slot in range(1, 16):
        stats(slot).start()

    def weigh_first(a, carry):
        here = block_lanes(a)
        shifted = ta[0:1, here] - local
        w2a[0:width, here] = (w1a[0:width, here].astype(F32) * shifted).astype(BF16)
        w2a[width:deep, here] = jnp.concatenate([three_rows(split3(shifted * sign), 0), none8], axis=0).astype(BF16)
        return carry

    lax.fori_loop(0, na, weigh_first, 0)

    def sum_second_again(pair, carry):
        sum_second(w2a, o2b, pair)
        return carry

    lax.fori_loop(0, SECOND_PAIRS, sum_second_again, 0)
    for b in second_others:
        total_second(b).wait_recv()

    def weigh_second(b, carry):
        here = block_lanes(b)
        shifted = tb[0:1, here] - local
        wb[width : 2 * width, here] = (wb[0:width, here].astype(F32) * shifted).astype(BF16)
        tail = sign8 + three_rows(split3(shifted * sign), 1)
        wb[2 * width : 2 * width + 16, here] = jnp.concatenate([tail, none8], axis=0).astype(BF16)
        return carry

    lax.fori_loop(0, nb, weigh_second, 0)
    inner = TWO_SIDED * 2 * both
    oa[:, 6 * both : 8 * both] = matmul_t(wb[:, 0:inner], km[6 * both : 8 * both, 0:inner])

    for slot in range(1, 16):
        stats(slot).wait_recv()
    every = stat_in[...]
    added = jnp.sum(every, axis=0)
    mean = added[0:1, 0:1] * (1.0 / 16.0)
    away = jnp.sum(jnp.square(every - mean), axis=0)
    spread = added[0:1, 64:65] + float(na * each) * away[0:1, 0:1]
    variance = 4.0 * spread / points**3 + 1e-08
    statistic = mean / points
    deviation = jnp.sqrt(variance)
    coef_a = 1.0 / (points * deviation)
    coef_b = -4.0 * statistic / (points**2 * (variance * deviation))
    objective_ref[...] = jnp.broadcast_to(statistic / deviation, objective_ref.shape)
    base = 2.0 * coef_a + 2.0 * coef_b * (local - mean)
    outer = sign * (-1.0 / width)

    def combine(value, shifted, plain, rho, weighted, tau):
        alpha = base + coef_b * shifted
        return (value * rho - plain) * (alpha * outer) + (value * tau - weighted) * (coef_b * outer)

    def gradient_first(a):
        here = block_lanes(a)
        low = 2 * width
        tau = oa[low + 1 : low + 2, here] + oa[low + 2 : low + 3, here] + oa[low + 3 : low + 4, here]
        return combine(
            at[:, here].astype(F32), ta[0:1, here] - local,
            oa[0:width, here], oa[low : low + 1, here], oa[width:low, here], tau,
        )

    def gradient_second(b):
        here = block_lanes(b)
        tau = o2b[width : width + 1, here] + o2b[width + 1 : width + 2, here] + o2b[width + 2 : width + 3, here]
        return combine(
            bt[0:width, here].astype(F32), tb[0:1, here] - local,
            o1b[0:width, here], o1b[width : width + 1, here], o2b[0:width, here], tau,
        )

    def finish_second(j, carry):
        b = nb - 1 - j

        @pl.when(b != OWN_SECOND)
        def _():
            gb[:, block_lanes(b)] = gradient_second(b).astype(BF16)
            return_second(b).start()

        return carry

    def finish_first(a):
        ga[:, block_lanes(a)] = gradient_first(a).astype(BF16)
        return_first(a).start()

    lax.fori_loop(0, nb, finish_second, 0)
    finish_first(6)
    finish_first(7)

    def first_sums(j, carry):
        ap = 2 - j
        here = lanes(ap, 2)
        oa[:, here] = matmul_t(wb[...], km[here, :])

        @pl.when(ap > 0)
        def _():
            finish_first(2 * ap)

        finish_first(2 * ap + 1)
        return carry

    lax.fori_loop(0, 3, first_sums, 0)
    result = gradient_first(OWN_FIRST) + gradient_second(OWN_SECOND)
    for a in first_others:
        return_first(a).wait_recv()
        result = result + g_in[a].astype(F32)
    for b in second_others:
        return_second(b).wait_recv()
        result = result + g_in[na + b].astype(F32)
    result = result.T
    grad_pool_ref[...] = result[0:each]
    grad_label_ref[...] = result[each:both]

    for a in first_others:
        for item in (gather_first, partial_first, total_first, return_first):
            item(a).wait_send()
    for b in second_others:
        for item in (gather_second, partial_second, total_second, return_second):
            item(b).wait_send()
    for slot in range(1, 16):
        stats(slot).wait_send()


def shards(pool, labeled):
    each, width = pool.shape
    both = 2 * each
    deep = width + 16
    na, nb = len(FIRST), len(SECOND)
    la, lb = na * both, nb * both
    dma = pltpu.SemaphoreType.DMA
    vmem = pl.BlockSpec(memory_space=pltpu.VMEM)
    scratch = [
        pltpu.VMEM((width, both), BF16),
        pltpu.VMEM((width, la), BF16),
        pltpu.VMEM((2 * width, lb), BF16),
        pltpu.VMEM((la, 2 * width), BF16),
        pltpu.VMEM((la, lb), BF16),
        pltpu.VMEM((la, 128), F32),
        pltpu.VMEM((16, lb), F32),
        pltpu.VMEM((8, la), F32),
        pltpu.VMEM((8, lb), F32),
        pltpu.VMEM((na + nb, 8, both), F32),
        pltpu.VMEM((8, both), F32),
        pltpu.VMEM((8, la), F32),
        pltpu.VMEM((8, lb), F32),
        pltpu.VMEM((deep, la), BF16),
        pltpu.VMEM((deep, la), BF16),
        pltpu.VMEM((width + deep, lb), BF16),
        pltpu.VMEM((deep, lb), F32),
        pltpu.VMEM((deep, lb), F32),
        pltpu.VMEM((width + deep, la), F32),
        pltpu.VMEM((width, la), BF16),
        pltpu.VMEM((width, lb), BF16),
        pltpu.VMEM((na + nb, width, both), BF16),
        pltpu.VMEM((8, 128), F32),
        pltpu.VMEM((16, 8, 128), F32),
    ]
    for _ in range(4):
        scratch += [dma((na,)), dma((na,)), dma((nb,)), dma((nb,))]
    scratch += [dma((16,)), dma((16,))]
    grad_pool, grad_label, objective = pl.pallas_call(
        kernel,
        out_shape=(
            jax.ShapeDtypeStruct((each, width), F32),
            jax.ShapeDtypeStruct((each, width), F32),
            jax.ShapeDtypeStruct((8, 128), F32),
        ),
        in_specs=[vmem, vmem],
        out_specs=(vmem, vmem, vmem),
        scratch_shapes=scratch,
        compiler_params=pltpu.CompilerParams(
            collective_id=0, has_side_effects=True, vmem_limit_bytes=60 * 2**20
        ),
    )(pool, labeled)
    return grad_pool, grad_label, objective[0, 0]


def solution(mesh):
    in_specs = (P(("row", "col"), None), P(("row", "col"), None))
    out_specs = (P(("row", "col"), None), P(("row", "col"), None), P())
    return jax.shard_map(shards, mesh=mesh, in_specs=in_specs, out_specs=out_specs, check_vma=False)
```

time: 84 us -> 68.3 us (0.81)
  Pallas kernels: 79.7 us -> 64 us
    pallas_call x1, Pallas kernels: 79.7 us -> 64 us  [shards(): pl.pallas_call(kernel, out_shape=(jax.ShapeDtypeStruct((each, width), F32...]
where the time goes in v2:
time: 68.3 us; the launch traced here: 68.1 us
  Pallas kernels  64 us (94%)
  local copies, waits for them, and re-layouts  3.4 us (5%)
    pallas_call x1, Pallas kernels, shards(): pl.pallas_call(kernel, out_shape=(jax.ShapeDtypeStruct((each, width), F32...  64 us
    unnamed x4, local copies, waits for them, and re-layouts  2.22 us

profile of v2, /device:TPU:1, one launch (start us, length us, event | category | flops | bytes accessed | tf_op | source)
XLA Modules:
  0.0 68.1 jit_solution(12986236630437381247)
XLA Ops:
  0.6 64.0 %shard_map.49 = (f32[192,128]{1,0:T(8,128)}, f32[192,128]{1,0:T(8,128)}, f32[8,128]{1,0:T(8,128)}) custom-call(bf16[192,128]{1,0:T(8,128)(2,1)} %pool_ref.1, bf16[192,128]{1,0:T(8,128)(2,1)} %label_ref.1), custom_call_target="tpu_custom_call" | custom-call | tf_op jit(solution)/shard_map/pallas_call | solution.py:454
  64.6 1.2 %slice.3 = f32[1,1]{1,0:T(1,128)} slice(f32[8,128]{1,0:T(8,128)} %get-tuple-element.8), slice={[0:1], [0:1]} | slice | bytes 8 | tf_op jit(solution)/shard_map/slice | solution.py:468
  65.8 0.0 copy-start
  65.8 1.6 %copy.7 = f32[192,128]{1,0:T(8,128)} copy(f32[192,128]{1,0:T(8,128)} %get-tuple-element.12) | data formatting | bytes 196608
  67.4 0.0 copy-done
  67.4 0.6 copy.8
Async XLA Ops:
  65.8 1.6 %copy-start = (f32[192,128]{1,0:T(8,128)S(1)}, f32[192,128]{1,0:T(8,128)}, u32[]{:S(2)}) copy-start(f32[192,128]{1,0:T(8,128)} %get-tuple-element.13) | copy-start | bytes 294916

commit v3 on v2

--- a/solution.py
+++ b/solution.py
@@ -12,9 +12,20 @@
 BF16 = jnp.bfloat16
 
 FIRST = tuple((dx, dk) for dx in range(4) for dk in range(2))
-SECOND = ((0, 1), (1, 0), (-1, -1), (-1, 1), (1, 2), (2, -1), (0, 0), (0, 2), (2, 0), (2, 2))
+SECOND = ((0, 1), (-1, 0), (1, 1), (-1, 1), (1, 2), (2, -1), (0, 0), (0, 2), (2, 0), (2, 2))
 OWN_FIRST = FIRST.index((0, 0))
 OWN_SECOND = SECOND.index((0, 0))
+RELAY = {
+    0: ((0, 1), (0, 1)),
+    1: ((-1, 0), (-1, 0)),
+    2: ((1, 0), (1, 0)),
+    3: ((-1, 0), (0, 1)),
+    7: ((0, 1), (0, 1)),
+    8: ((-1, 0), (-1, 0)),
+    4: ((1, 0), (1, 0)),
+    5: ((0, -1), (0, -1)),
+    9: ((-1, 1), (-1, 1)),
+}
 TWO_SIDED = 3
 SECOND_PAIRS = len(SECOND) // 2
 
@@ -53,7 +64,7 @@
 
 def kernel(
     pool_ref, label_ref, grad_pool_ref, grad_label_ref, objective_ref,
-    own, at, bt, za, km, acc_a, acc_b, part_a, part_b, part_in, t_own, ta, tb,
+    own, at, bt, za, km, acc_a, acc_b, part_a, part_b, first_in, second_in, sum_b, sum_b_in, t_own, ta, tb,
     w1a, w2a, wb, o1b, o2b, oa, ga, gb, g_in, stat_out, stat_in,
     ga_send, ga_recv, gb_send, gb_recv, pa_send, pa_recv, pb_send, pb_recv,
     ta_send, ta_recv, tb_send, tb_recv, ra_send, ra_recv, rb_send, rb_recv, st_send, st_recv,
@@ -85,6 +96,7 @@
 
     first_others = [a for a in range(na) if a != OWN_FIRST]
     second_others = [b for b in range(nb) if b != OWN_SECOND]
+    shared = range(2 * TWO_SIDED)
 
     def lanes(index, count=1):
         return pl.ds(pl.multiple_of(index * both * count, both * count), both * count)
@@ -95,19 +107,34 @@
     def gather_first(a):
         return copy(own, at.at[:, block_lanes(a)], ga_send.at[a], ga_recv.at[a], from_first(a))
 
+    def forward(a):
+        return copy(
+            at.at[:, block_lanes(a - 1)], at.at[:, block_lanes(a)], ga_send.at[a], ga_recv.at[a],
+            device(x, y, z, core + 1),
+        )
+
     def gather_second(b):
+        if b in (0, 1):
+            source = own
+        else:
+            at_neighbour = {2: 0, 3: jnp.where(core == 0, 0, 1), 4: 7, 5: 8, 7: 0, 8: 1, 9: 3}[b]
+            source = bt.at[pl.ds(0, width), block_lanes(at_neighbour)]
+        first, other = RELAY[b]
+        dy = jnp.where(core == 0, first[0], other[0])
+        dz = jnp.where(core == 0, first[1], other[1])
         return copy(
-            own, bt.at[pl.ds(0, width), block_lanes(b)], gb_send.at[b], gb_recv.at[b], from_second(b)
+            source, bt.at[pl.ds(0, width), block_lanes(b)], gb_send.at[b], gb_recv.at[b],
+            device(x, y - dy, z - dz, core),
         )
 
     def partial_first(a):
-        return copy(part_a.at[:, block_lanes(a)], part_in.at[a], pa_send.at[a], pa_recv.at[a], to_first(a))
+        return copy(part_a, first_in.at[a], pa_send.at[a], pa_recv.at[a], from_first(a))
 
     def partial_second(b):
-        return copy(part_b.at[:, block_lanes(b)], part_in.at[na + b], pb_send.at[b], pb_recv.at[b], to_second(b))
+        return copy(part_b.at[:, block_lanes(b)], second_in.at[b], pb_send.at[b], pb_recv.at[b], to_second(b))
 
     def total_first(a):
-        return copy(t_own, ta.at[:, block_lanes(a)], ta_send.at[a], ta_recv.at[a], from_first(a))
+        return copy(sum_b, sum_b_in.at[a], ta_send.at[a], ta_recv.at[a], from_first(a))
 
     def total_second(b):
         return copy(t_own, tb.at[:, block_lanes(b)], tb_send.at[b], tb_recv.at[b], from_second(b))
@@ -142,20 +169,11 @@
 
     pl.semaphore_wait(barrier, len(partners))
 
+    for a in (2, 6, 1):
+        gather_first(a).start()
     for b in (0, 1):
         gather_second(b).start()
-    for a in (1, 2, 3):
-        gather_first(a).start()
-    for b in (2, 3):
-        gather_second(b).start()
-    for a in (6, 7):
-        gather_first(a).start()
-    for b in (7, 4, 5):
-        gather_second(b).start()
-    for a in (4, 5):
-        gather_first(a).start()
-    for b in (8, 9):
-        gather_second(b).start()
+    gather_first(4).start()
 
     place8 = lax.broadcasted_iota(jnp.int32, (8, both), 0)
     none8 = jnp.zeros((8, both), F32)
@@ -189,110 +207,123 @@
     scale = math.log2(math.e) / width
     tile_sign = sign[:, 128:256]
 
-    def order(i):
-        return i + jnp.where(i == 2, 1, 0) - jnp.where(i == 3, 1, 0)
-
-    def sum_second(w, out, pair):
-        here = lanes(pair, 2)
-
-        @pl.when(pair < TWO_SIDED)
-        def _():
+    def sum_second(w, out):
+        def body(pair, carry):
+            here = lanes(pair, 2)
             out[:, here] = matmul(w[...], km[:, here])
-
-        @pl.when(pair >= TWO_SIDED)
-        def _():
-            out[:, here] = matmul(w[:, 2 * both : 4 * both], km[2 * both : 4 * both, here])
-
-    def second_step(i, carry):
-        pair = order(i)
-
-        @pl.when(i > 0)
-        def _():
-            sum_second(w1a, o1b, order(i - 1))
-
-        def await_second(b):
-            @pl.when(b != OWN_SECOND)
-            def _():
-                gather_second(b).wait_recv()
-
-            take_second(b)
-
-        await_second(2 * pair)
-        await_second(2 * pair + 1)
+            return carry
+
+        lax.fori_loop(0, TWO_SIDED, body, 0)
+
+    def turn(expected, following):
+        for b in expected:
+            gather_second(b).wait_recv()
+        for b in following:
+            gather_second(b).start()
+
+    def once(t, steps, action):
+        chosen = t == steps[0]
+        for step in steps[1:]:
+            chosen = chosen | (t == step)
+        pl.when(chosen)(action)
+
+    def kernel_step(t, carry):
+        late = t - 8
+        pair = jnp.where(t < 3, 0, jnp.where(t < 6, 1, jnp.where(t < 8, t - 6, pick(late // 4, (3, 2, 4)))))
+        ap = jnp.where(t < 6, pick(t % 3, (0, 1, 3)), jnp.where(t < 8, 2, late % 4))
+
+        def relay_first(a):
+            gather_first(a).wait_recv()
+            forward(a + 1).start()
+
+        once(t, (0,), lambda: turn((0, 1), (2, 3, 7, 8)))
+        once(t, (3,), lambda: turn((2, 3, 7, 8), (4, 5, 9)))
+        once(t, (12,), lambda: turn((4, 5), ()))
+        once(t, (16,), lambda: turn((9,), ()))
+        once(t, (0,), lambda: relay_first(2))
+        once(t, (1,), lambda: relay_first(6))
+        once(t, (4,), lambda: relay_first(4))
+
+        def new_second():
+            take_second(2 * pair)
+            take_second(2 * pair + 1)
+
+        def new_first():
+            gather_first(2 * ap + 1).wait_recv()
+            take_first(2 * ap)
+            take_first(2 * ap + 1)
+
+        once(t, (0, 3, 8, 12, 16), new_second)
+        once(t, (0, 1, 2, 6), new_first)
         wide = lanes(pair, 2)
-
-        def first_step(ap, carry):
-            @pl.when(i == 0)
-            def _():
-                @pl.when(ap > 0)
-                def _():
-                    gather_first(2 * ap).wait_recv()
-
-                gather_first(2 * ap + 1).wait_recv()
-                take_first(2 * ap)
-                take_first(2 * ap + 1)
-
-            here = lanes(ap, 2)
-            product = matmul(za[here, :], bt[:, wide])
-            value = jnp.exp2(product * scale)
-            km[here, wide] = value.astype(BF16)
-            tiles = [value[:, 128 * j : 128 * (j + 1)] for j in range(6)]
-            across = (tiles[0] - tiles[2]) + (tiles[3] - tiles[5]) + (tiles[1] + tiles[4]) * tile_sign
-            acc_a[here, :] += across
-            parts = [
-                jnp.sum(value[each * j : each * (j + 1)].reshape(each // 8, 8, 2 * both), axis=0) for j in range(4)
-            ]
-            unused = (pair >= TWO_SIDED) & (ap != 1)
-            to = pl.multiple_of(jnp.where(unused, 8, 0), 8)
-            acc_b[pl.ds(to, 8), wide] += (parts[0] - parts[1]) + (parts[2] - parts[3])
-            return carry
-
-        lax.fori_loop(0, jnp.where(pair < TWO_SIDED, 4, 3), first_step, 0)
-
-        for b in (2 * pair, 2 * pair + 1):
-            here = block_lanes(b)
-            part_b[:, here] = jnp.broadcast_to(jnp.sum(acc_b[0:8, here], axis=0, keepdims=True) * sign, (8, both))
-
-            @pl.when(b != OWN_SECOND)
-            def _():
+        here = lanes(ap, 2)
+        product = matmul(za[here, :], bt[:, wide])
+        value = jnp.exp2(product * scale)
+        km[here, wide] = value.astype(BF16)
+        tiles = [value[:, 128 * j : 128 * (j + 1)] for j in range(6)]
+        across = (tiles[0] - tiles[2]) + (tiles[3] - tiles[5]) + (tiles[1] + tiles[4]) * tile_sign
+        acc_a[here, :] += across
+        parts = [
+            jnp.sum(value[each * j : each * (j + 1)].reshape(each // 8, 8, 2 * both), axis=0) for j in range(4)
+        ]
+        acc_b[:, lanes(jnp.minimum(pair, TWO_SIDED), 2)] += (parts[0] - parts[1]) + (parts[2] - parts[3])
+
+        def second_done():
+            for b in (2 * pair, 2 * pair + 1):
+                here = block_lanes(b)
+                total = jnp.sum(acc_b[:, here], axis=0, keepdims=True) * sign
+                part_b[:, here] = jnp.broadcast_to(total, (8, both))
                 partial_second(b).start()
 
+        once(t, (6, 7, 15), second_done)
         return carry
 
-    lax.fori_loop(0, SECOND_PAIRS, second_step, 0)
-
-    for a in (4, 5, 2, 3, 6, 7, 1, 0):
-        here = pl.ds(a * both, both)
-        total = jnp.sum(acc_a[here, :].T, axis=0, keepdims=True) * sign
-        part_a[:, here] = jnp.broadcast_to(total, (8, both))
-        if a != OWN_FIRST:
-            partial_first(a).start()
-    sum_second(w1a, o1b, SECOND_PAIRS - 1)
-
-    total = part_a[:, pl.ds(OWN_FIRST * both, both)] + part_b[:, pl.ds(OWN_SECOND * both, both)]
-    for b in second_others:
+    lax.fori_loop(0, 4 * SECOND_PAIRS, kernel_step, 0)
+
+    rows8 = none8
+    for a in range(na):
+        rows8 = jnp.where(place8 == a, jnp.sum(acc_a[a * both : (a + 1) * both, :].T, axis=0, keepdims=True), rows8)
+    part_a[...] = rows8 * sign
+    for a in first_others:
+        partial_first(a).start()
+    got = none8
+    for b in shared:
         partial_second(b).wait_recv()
-        total = total + part_in[na + b]
+        got = got + second_in[b]
+    sum_b[...] = got
+    for a in first_others:
+        total_first(a).start()
+    sum_second(w1a, o1b)
+
+    def seen_from(value, a):
+        dx, dk = FIRST[a]
+        if dk:
+            value = jnp.where(place8 % 2 == 0, pltpu.roll(value, 7, 0), pltpu.roll(value, 1, 0))
+        return pltpu.roll(value, 2 * dx, 0) if dx else value
+
+    total = part_a[...]
     for a in first_others:
         partial_first(a).wait_recv()
-        total = total + part_in[a]
+        total = total + seen_from(first_in[a], a)
+    total = total + jnp.where(place8 == OWN_FIRST, got, 0.0)
+    for a in first_others:
+        total_first(a).wait_recv()
+        total = total + jnp.where(place8 == a, sum_b_in[a], 0.0)
     total = total + pltpu.roll(total, each, 1)
-    t_own[...] = total
-    ta[:, pl.ds(OWN_FIRST * both, both)] = total
-    tb[:, pl.ds(OWN_SECOND * both, both)] = total
-    for a in first_others:
-        total_first(a).start()
+    for a in range(na):
+        ta[:, a * both : (a + 1) * both] = jnp.broadcast_to(total[a : a + 1], (8, both))
+    mine = jnp.broadcast_to(total[OWN_FIRST : OWN_FIRST + 1], (8, both))
+    t_own[...] = mine
+    tb[:, pl.ds(OWN_SECOND * both, both)] = mine
     for b in second_others:
         total_second(b).start()
-    for a in first_others:
-        total_first(a).wait_recv()
 
     line = ta[0:1, :]
     local = jnp.sum(line, axis=1, keepdims=True) / (na * both)
     spread = 0.5 * jnp.sum(jnp.square(line - local), axis=1, keepdims=True)
-    shared = jnp.where(lax.broadcasted_iota(jnp.int32, (8, 128), 1) < 64, local, spread)
-    stat_out[...] = shared
-    stat_in[0] = shared
+    told = jnp.where(lax.broadcasted_iota(jnp.int32, (8, 128), 1) < 64, local, spread)
+    stat_out[...] = told
+    stat_in[0] = told
     for slot in range(1, 16):
         stats(slot).start()
 
@@ -305,11 +336,7 @@
 
     lax.fori_loop(0, na, weigh_first, 0)
 
-    def sum_second_again(pair, carry):
-        sum_second(w2a, o2b, pair)
-        return carry
-
-    lax.fori_loop(0, SECOND_PAIRS, sum_second_again, 0)
+    sum_second(w2a, o2b)
     for b in second_others:
         total_second(b).wait_recv()
 
@@ -322,9 +349,13 @@
         return carry
 
     lax.fori_loop(0, nb, weigh_second, 0)
-    inner = TWO_SIDED * 2 * both
-    oa[:, 6 * both : 8 * both] = matmul_t(wb[:, 0:inner], km[6 * both : 8 * both, 0:inner])
-
+
+    def first_sums(ap, carry):
+        here = lanes(ap, 2)
+        oa[:, here] = matmul_t(wb[...], km[here, :])
+        return carry
+
+    first_sums(3, 0)
     for slot in range(1, 16):
         stats(slot).wait_recv()
     every = stat_in[...]
@@ -363,41 +394,34 @@
         )
 
     def finish_second(j, carry):
-        b = nb - 1 - j
-
-        @pl.when(b != OWN_SECOND)
-        def _():
-            gb[:, block_lanes(b)] = gradient_second(b).astype(BF16)
-            return_second(b).start()
-
+        b = 2 * TWO_SIDED - 1 - j
+        gb[:, block_lanes(b)] = gradient_second(b).astype(BF16)
+        return_second(b).start()
         return carry
 
     def finish_first(a):
         ga[:, block_lanes(a)] = gradient_first(a).astype(BF16)
         return_first(a).start()
 
-    lax.fori_loop(0, nb, finish_second, 0)
-    finish_first(6)
-    finish_first(7)
-
-    def first_sums(j, carry):
-        ap = 2 - j
-        here = lanes(ap, 2)
-        oa[:, here] = matmul_t(wb[...], km[here, :])
-
-        @pl.when(ap > 0)
+    def finish_and_sum(j, carry):
+        ap = 3 - j
+        finish_first(2 * ap)
+        finish_first(2 * ap + 1)
+
+        @pl.when(j == 0)
         def _():
-            finish_first(2 * ap)
-
-        finish_first(2 * ap + 1)
+            lax.fori_loop(0, 2 * TWO_SIDED, finish_second, 0)
+
+        first_sums(ap - 1, 0)
         return carry
 
-    lax.fori_loop(0, 3, first_sums, 0)
-    result = gradient_first(OWN_FIRST) + gradient_second(OWN_SECOND)
+    lax.fori_loop(0, 3, finish_and_sum, 0)
+    finish_first(1)
+    result = gradient_first(OWN_FIRST)
     for a in first_others:
         return_first(a).wait_recv()
         result = result + g_in[a].astype(F32)
-    for b in second_others:
+    for b in shared:
         return_second(b).wait_recv()
         result = result + g_in[na + b].astype(F32)
     result = result.T
@@ -405,10 +429,13 @@
     grad_label_ref[...] = result[each:both]
 
     for a in first_others:
-        for item in (gather_first, partial_first, total_first, return_first):
+        for item in (gather_first if a in (1, 2, 4, 6) else forward, partial_first, total_first, return_first):
             item(a).wait_send()
     for b in second_others:
-        for item in (gather_second, partial_second, total_second, return_second):
+        for item in (gather_second, total_second):
+            item(b).wait_send()
+    for b in shared:
+        for item in (partial_second, return_second):
             item(b).wait_send()
     for slot in range(1, 16):
         stats(slot).wait_send()
@@ -419,7 +446,7 @@
     both = 2 * each
     deep = width + 16
     na, nb = len(FIRST), len(SECOND)
-    la, lb = na * both, nb * both
+    la, lb, ls = na * both, nb * both, 2 * TWO_SIDED * both
     dma = pltpu.SemaphoreType.DMA
     vmem = pl.BlockSpec(memory_space=pltpu.VMEM)
     scratch = [
@@ -429,21 +456,24 @@
         pltpu.VMEM((la, 2 * width), BF16),
         pltpu.VMEM((la, lb), BF16),
         pltpu.VMEM((la, 128), F32),
-        pltpu.VMEM((16, lb), F32),
-        pltpu.VMEM((8, la), F32),
-        pltpu.VMEM((8, lb), F32),
-        pltpu.VMEM((na + nb, 8, both), F32),
+        pltpu.VMEM((8, ls + 2 * both), F32),
+        pltpu.VMEM((8, both), F32),
+        pltpu.VMEM((8, ls), F32),
+        pltpu.VMEM((na, 8, both), F32),
+        pltpu.VMEM((2 * TWO_SIDED, 8, both), F32),
+        pltpu.VMEM((8, both), F32),
+        pltpu.VMEM((na, 8, both), F32),
         pltpu.VMEM((8, both), F32),
         pltpu.VMEM((8, la), F32),
         pltpu.VMEM((8, lb), F32),
         pltpu.VMEM((deep, la), BF16),
         pltpu.VMEM((deep, la), BF16),
         pltpu.VMEM((width + deep, lb), BF16),
-        pltpu.VMEM((deep, lb), F32),
-        pltpu.VMEM((deep, lb), F32),
+        pltpu.VMEM((deep, ls), F32),
+        pltpu.VMEM((deep, ls), F32),
         pltpu.VMEM((width + deep, la), F32),
         pltpu.VMEM((width, la), BF16),
-        pltpu.VMEM((width, lb), BF16),
+        pltpu.VMEM((width, ls), BF16),
         pltpu.VMEM((na + nb, width, both), BF16),
         pltpu.VMEM((8, 128), F32),
         pltpu.VMEM((16, 8, 128), F32),
@@ -465,7 +495,23 @@
             collective_id=0, has_side_effects=True, vmem_limit_bytes=60 * 2**20
         ),
     )(pool, labeled)
-    return grad_pool, grad_label, objective[0, 0]
+
+    def hand_on(pool_in, label_in, objective_in, pool_out, label_out, objective_out):
+        pool_out[...] = pool_in[...]
+        label_out[...] = label_in[...]
+        objective_out[0, 0] = objective_in[0, 0]
+
+    grad_pool, grad_label, objective = pl.pallas_call(
+        hand_on,
+        out_shape=(
+            jax.ShapeDtypeStruct((each, width), F32),
+            jax.ShapeDtypeStruct((each, width), F32),
+            jax.ShapeDtypeStruct((1, 1), F32),
+        ),
+        in_specs=[vmem, vmem, vmem],
+        out_specs=(vmem, vmem, pl.BlockSpec(memory_space=pltpu.SMEM)),
+    )(grad_pool, grad_label, objective)
+    return grad_pool, grad_label, objective.reshape(())
 
 
 def solution(mesh):

time: 68.3 us -> 61.4 us (0.90)
  Pallas kernels: 64 us -> 60.5 us
  local copies, waits for them, and re-layouts: 3.4 us -> 0 us
    pallas_call x1, Pallas kernels: 64 us -> 58.9 us  [shards(): pl.pallas_call(kernel, out_shape=(jax.ShapeDtypeStruct((each, width), F32...]
    unnamed x4 -> x0, local copies, waits for them, and re-layouts: 2.22 us -> none
    pallas_call x0 -> x1, Pallas kernels: none -> 1.63 us  [shards(): pl.pallas_call(hand_on, out_shape=(jax.ShapeDtypeStruct((each, width), F3...]
    slice x1 -> x0, local copies, waits for them, and re-layouts: 1.19 us -> none  [shards(): return (grad_pool, grad_label, objective[0, 0])]
where the time goes in v3:
time: 61.4 us; the launch traced here: 61.2 us
  Pallas kernels  60.5 us (99%)
  between operations  0.64 us (1%)
    pallas_call x1, Pallas kernels, shards(): pl.pallas_call(kernel, out_shape=(jax.ShapeDtypeStruct((each, width), F32...  58.9 us
    pallas_call x1, Pallas kernels, shards(): pl.pallas_call(hand_on, out_shape=(jax.ShapeDtypeStruct((each, width), F3...  1.63 us

profile of v3, /device:TPU:1, one launch (start us, length us, event | category | flops | bytes accessed | tf_op | source)
XLA Modules:
  0.0 61.2 jit_solution(10375229328699012250)
XLA Ops:
  0.6 58.9 %shard_map.49 = (f32[192,128]{1,0:T(8,128)}, f32[192,128]{1,0:T(8,128)}, f32[8,128]{1,0:T(8,128)}) custom-call(bf16[192,128]{1,0:T(8,128)(2,1)} %pool_ref.1, bf16[192,128]{1,0:T(8,128)(2,1)} %label_ref.1), custom_call_target="tpu_custom_call" | custom-call | tf_op jit(solution)/shard_map/pallas_call | solution.py:484
  59.5 1.6 %shard_map.50 = (f32[192,128]{1,0:T(8,128)}, f32[192,128]{1,0:T(8,128)}, f32[1,1]{1,0:T(1,128)}) custom-call(f32[192,128]{1,0:T(8,128)} %get-tuple-element.9.pool_in, f32[192,128]{1,0:T(8,128)} %get-tuple-element.10.label_in, f32[8,128]{1,0:T(8,128)} %get-tuple-element.11.objective_in), custom_call_target="tpu_custom_call" | custom-call | tf_op jit(solution)/shard_map/pallas_call | solution.py:504

commit v4 on v3

--- a/solution.py
+++ b/solution.py
@@ -24,7 +24,7 @@
     8: ((-1, 0), (-1, 0)),
     4: ((1, 0), (1, 0)),
     5: ((0, -1), (0, -1)),
-    9: ((-1, 1), (-1, 1)),
+    9: ((0, 2), (2, 0)),
 }
 TWO_SIDED = 3
 SECOND_PAIRS = len(SECOND) // 2
@@ -64,10 +64,10 @@
 
 def kernel(
     pool_ref, label_ref, grad_pool_ref, grad_label_ref, objective_ref,
-    own, at, bt, za, km, acc_a, acc_b, part_a, part_b, first_in, second_in, sum_b, sum_b_in, t_own, ta, tb,
+    rows_in, own, at, bt, za, km, acc_a, acc_b, part_a, part_b, first_in, second_in, sum_b, sum_b_in, t_own, ta, tb,
     w1a, w2a, wb, o1b, o2b, oa, ga, gb, g_in, stat_out, stat_in,
     ga_send, ga_recv, gb_send, gb_recv, pa_send, pa_recv, pb_send, pb_recv,
-    ta_send, ta_recv, tb_send, tb_recv, ra_send, ra_recv, rb_send, rb_recv, st_send, st_recv,
+    ta_send, ta_recv, tb_send, tb_recv, ra_send, ra_recv, rb_send, rb_recv, st_send, st_recv, read_sem,
 ):
     width = pool_ref.shape[1]
     each = pool_ref.shape[0]
@@ -117,7 +117,7 @@
         if b in (0, 1):
             source = own
         else:
-            at_neighbour = {2: 0, 3: jnp.where(core == 0, 0, 1), 4: 7, 5: 8, 7: 0, 8: 1, 9: 3}[b]
+            at_neighbour = {2: 0, 3: jnp.where(core == 0, 0, 1), 4: 7, 5: 8, 7: 0, 8: 1, 9: jnp.where(core == 0, 8, 7)}[b]
             source = bt.at[pl.ds(0, width), block_lanes(at_neighbour)]
         first, other = RELAY[b]
         dy = jnp.where(core == 0, first[0], other[0])
@@ -149,16 +149,24 @@
         target = device(x, y - slot // 4, z - slot % 4, core)
         return copy(stat_out, stat_in.at[slot], st_send.at[slot], st_recv.at[slot], target)
 
-    partners = [(dx, 0, 0, dk) for dx, dk in FIRST if (dx, dk) != (0, 0)]
-    partners += [(0, slot // 4, slot % 4, 0) for slot in range(1, 16)]
+    partners = [(0, 0, 0, 1), (1, 0, 0, 0), (3, 0, 0, 0), (2, 0, 0, 0)]
+    partners += [(0, 1, 0, 0), (0, 3, 0, 0), (0, 0, 1, 0), (0, 0, 3, 0)]
     barrier = pltpu.get_barrier_semaphore()
     for dx, dy, dz, dk in partners:
         pl.semaphore_signal(
             barrier, inc=1, device_id=device(x + dx, y + dy, z + dz, core + dk), device_id_type=MESH
         )
 
+    reads = [
+        pltpu.make_async_copy(pool_ref, rows_in.at[pl.ds(0, each)], read_sem.at[0]),
+        pltpu.make_async_copy(label_ref, rows_in.at[pl.ds(each, each)], read_sem.at[1]),
+    ]
+    for item in reads:
+        item.start()
     sign = jnp.where(lax.broadcasted_iota(jnp.int32, (1, both), 1) < each, 1.0, -1.0).astype(F32)
-    rows = jnp.concatenate([pool_ref[...].astype(F32), label_ref[...].astype(F32)], axis=0)
+    for item in reads:
+        item.wait()
+    rows = rows_in[...].astype(F32)
     block = rows.T.astype(BF16)
     own[...] = block
     at[:, pl.ds(OWN_FIRST * both, both)] = block
@@ -315,7 +323,7 @@
     mine = jnp.broadcast_to(total[OWN_FIRST : OWN_FIRST + 1], (8, both))
     t_own[...] = mine
     tb[:, pl.ds(OWN_SECOND * both, both)] = mine
-    for b in second_others:
+    for b in (9, 4, 5, 8, 7, 3, 2, 1, 0):
         total_second(b).start()
 
     line = ta[0:1, :]
@@ -450,6 +458,7 @@
     dma = pltpu.SemaphoreType.DMA
     vmem = pl.BlockSpec(memory_space=pltpu.VMEM)
     scratch = [
+        pltpu.VMEM((both, width), BF16),
         pltpu.VMEM((width, both), BF16),
         pltpu.VMEM((width, la), BF16),
         pltpu.VMEM((2 * width, lb), BF16),
@@ -480,7 +489,7 @@
     ]
     for _ in range(4):
         scratch += [dma((na,)), dma((na,)), dma((nb,)), dma((nb,))]
-    scratch += [dma((16,)), dma((16,))]
+    scratch += [dma((16,)), dma((16,)), dma((2,))]
     grad_pool, grad_label, objective = pl.pallas_call(
         kernel,
         out_shape=(
@@ -488,7 +497,7 @@
             jax.ShapeDtypeStruct((each, width), F32),
             jax.ShapeDtypeStruct((8, 128), F32),
         ),
-        in_specs=[vmem, vmem],
+        in_specs=[pl.BlockSpec(memory_space=pl.ANY)] * 2,
         out_specs=(vmem, vmem, vmem),
         scratch_shapes=scratch,
         compiler_params=pltpu.CompilerParams(

time: 61.4 us -> 59.4 us (0.967)
  Pallas kernels: 60.5 us -> 58.6 us
    pallas_call x1, Pallas kernels: 58.9 us -> 57 us  [shards(): pl.pallas_call(kernel, out_shape=(jax.ShapeDtypeStruct((each, width), F32...]
where the time goes in v4:
time: 59.4 us; the launch traced here: 59.2 us
  Pallas kernels  58.6 us (99%)
  between operations  0.64 us (1%)
    pallas_call x1, Pallas kernels, shards(): pl.pallas_call(kernel, out_shape=(jax.ShapeDtypeStruct((each, width), F32...  57 us
    pallas_call x1, Pallas kernels, shards(): pl.pallas_call(hand_on, out_shape=(jax.ShapeDtypeStruct((each, width), F3...  1.63 us

profile of v4, /device:TPU:1, one launch (start us, length us, event | category | flops | bytes accessed | tf_op | source)
XLA Modules:
  0.0 59.2 jit_solution(1492194192602643867)
XLA Ops:
  0.6 57.0 %shard_map.49 = (f32[192,128]{1,0:T(8,128)}, f32[192,128]{1,0:T(8,128)}, f32[8,128]{1,0:T(8,128)}) custom-call(bf16[192,128]{1,0:T(8,128)(2,1)} %pool_ref.1, bf16[192,128]{1,0:T(8,128)(2,1)} %label_ref.1), custom_call_target="tpu_custom_call" | custom-call | tf_op jit(solution)/shard_map/pallas_call | solution.py:493
  57.6 1.6 %shard_map.50 = (f32[192,128]{1,0:T(8,128)}, f32[192,128]{1,0:T(8,128)}, f32[1,1]{1,0:T(1,128)}) custom-call(f32[192,128]{1,0:T(8,128)} %get-tuple-element.9.pool_in, f32[192,128]{1,0:T(8,128)} %get-tuple-element.10.label_in, f32[8,128]{1,0:T(8,128)} %get-tuple-element.11.objective_in), custom_call_target="tpu_custom_call" | custom-call | tf_op jit(solution)/shard_map/pallas_call | solution.py:513

commit v5 on v4

--- a/solution.py
+++ b/solution.py
@@ -280,7 +280,7 @@
             for b in (2 * pair, 2 * pair + 1):
                 here = block_lanes(b)
                 total = jnp.sum(acc_b[:, here], axis=0, keepdims=True) * sign
-                part_b[:, here] = jnp.broadcast_to(total, (8, both))
+                part_b[:, here] = total
                 partial_second(b).start()
 
         once(t, (6, 7, 15), second_done)
@@ -294,7 +294,7 @@
     part_a[...] = rows8 * sign
     for a in first_others:
         partial_first(a).start()
-    got = none8
+    got = jnp.zeros((1, both), F32)
     for b in shared:
         partial_second(b).wait_recv()
         got = got + second_in[b]
@@ -320,7 +320,7 @@
     total = total + pltpu.roll(total, each, 1)
     for a in range(na):
         ta[:, a * both : (a + 1) * both] = jnp.broadcast_to(total[a : a + 1], (8, both))
-    mine = jnp.broadcast_to(total[OWN_FIRST : OWN_FIRST + 1], (8, both))
+    mine = total[OWN_FIRST : OWN_FIRST + 1]
     t_own[...] = mine
     tb[:, pl.ds(OWN_SECOND * both, both)] = mine
     for b in (9, 4, 5, 8, 7, 3, 2, 1, 0):
@@ -329,7 +329,7 @@
     line = ta[0:1, :]
     local = jnp.sum(line, axis=1, keepdims=True) / (na * both)
     spread = 0.5 * jnp.sum(jnp.square(line - local), axis=1, keepdims=True)
-    told = jnp.where(lax.broadcasted_iota(jnp.int32, (8, 128), 1) < 64, local, spread)
+    told = jnp.where(lax.broadcasted_iota(jnp.int32, (1, 128), 1) < 64, local, spread)
     stat_out[...] = told
     stat_in[0] = told
     for slot in range(1, 16):
@@ -363,7 +363,7 @@
         oa[:, here] = matmul_t(wb[...], km[here, :])
         return carry
 
-    first_sums(3, 0)
+    first_sums(2, 0)
     for slot in range(1, 16):
         stats(slot).wait_recv()
     every = stat_in[...]
@@ -412,7 +412,7 @@
         return_first(a).start()
 
     def finish_and_sum(j, carry):
-        ap = 3 - j
+        ap = pick(j, (2, 3, 1))
         finish_first(2 * ap)
         finish_first(2 * ap + 1)
 
@@ -420,18 +420,18 @@
         def _():
             lax.fori_loop(0, 2 * TWO_SIDED, finish_second, 0)
 
-        first_sums(ap - 1, 0)
+        first_sums(pick(j, (3, 1, 0)), 0)
         return carry
 
     lax.fori_loop(0, 3, finish_and_sum, 0)
     finish_first(1)
     result = gradient_first(OWN_FIRST)
-    for a in first_others:
-        return_first(a).wait_recv()
-        result = result + g_in[a].astype(F32)
     for b in shared:
         return_second(b).wait_recv()
         result = result + g_in[na + b].astype(F32)
+    for a in (1, 4, 5, 6, 7, 2, 3):
+        return_first(a).wait_recv()
+        result = result + g_in[a].astype(F32)
     result = result.T
     grad_pool_ref[...] = result[0:each]
     grad_label_ref[...] = result[each:both]
@@ -467,14 +467,14 @@
         pltpu.VMEM((la, 128), F32),
         pltpu.VMEM((8, ls + 2 * both), F32),
         pltpu.VMEM((8, both), F32),
-        pltpu.VMEM((8, ls), F32),
+        pltpu.VMEM((1, ls), F32),
         pltpu.VMEM((na, 8, both), F32),
-        pltpu.VMEM((2 * TWO_SIDED, 8, both), F32),
-        pltpu.VMEM((8, both), F32),
-        pltpu.VMEM((na, 8, both), F32),
-        pltpu.VMEM((8, both), F32),
+        pltpu.VMEM((2 * TWO_SIDED, 1, both), F32),
+        pltpu.VMEM((1, both), F32),
+        pltpu.VMEM((na, 1, both), F32),
+        pltpu.VMEM((1, both), F32),
         pltpu.VMEM((8, la), F32),
-        pltpu.VMEM((8, lb), F32),
+        pltpu.VMEM((1, lb), F32),
         pltpu.VMEM((deep, la), BF16),
         pltpu.VMEM((deep, la), BF16),
         pltpu.VMEM((width + deep, lb), BF16),
@@ -484,8 +484,8 @@
         pltpu.VMEM((width, la), BF16),
         pltpu.VMEM((width, ls), BF16),
         pltpu.VMEM((na + nb, width, both), BF16),
-        pltpu.VMEM((8, 128), F32),
-        pltpu.VMEM((16, 8, 128), F32),
+        pltpu.VMEM((1, 128), F32),
+        pltpu.VMEM((16, 1, 128), F32),
     ]
     for _ in range(4):
         scratch += [dma((na,)), dma((na,)), dma((nb,)), dma((nb,))]

time: 59.4 us -> 56.8 us (0.956)
  Pallas kernels: 58.6 us -> 56 us
    pallas_call x1, Pallas kernels: 57 us -> 54.3 us  [shards(): pl.pallas_call(kernel, out_shape=(jax.ShapeDtypeStruct((each, width), F32...]
where the time goes in v5:
time: 56.8 us; the launch traced here: 56.6 us
  Pallas kernels  56 us (99%)
  between operations  0.64 us (1%)
    pallas_call x1, Pallas kernels, shards(): pl.pallas_call(kernel, out_shape=(jax.ShapeDtypeStruct((each, width), F32...  54.3 us
    pallas_call x1, Pallas kernels, shards(): pl.pallas_call(hand_on, out_shape=(jax.ShapeDtypeStruct((each, width), F3...  1.63 us

profile of v5, /device:TPU:1, one launch (start us, length us, event | category | flops | bytes accessed | tf_op | source)
XLA Modules:
  0.0 56.6 jit_solution(1692654793273580718)
XLA Ops:
  0.6 54.3 %shard_map.49 = (f32[192,128]{1,0:T(8,128)}, f32[192,128]{1,0:T(8,128)}, f32[8,128]{1,0:T(8,128)}) custom-call(bf16[192,128]{1,0:T(8,128)(2,1)} %pool_ref.1, bf16[192,128]{1,0:T(8,128)(2,1)} %label_ref.1), custom_call_target="tpu_custom_call" | custom-call | tf_op jit(solution)/shard_map/pallas_call | solution.py:493
  55.0 1.6 %shard_map.50 = (f32[192,128]{1,0:T(8,128)}, f32[192,128]{1,0:T(8,128)}, f32[1,1]{1,0:T(1,128)}) custom-call(f32[192,128]{1,0:T(8,128)} %get-tuple-element.9.pool_in, f32[192,128]{1,0:T(8,128)} %get-tuple-element.10.label_in, f32[8,128]{1,0:T(8,128)} %get-tuple-element.11.objective_in), custom_call_target="tpu_custom_call" | custom-call | tf_op jit(solution)/shard_map/pallas_call | solution.py:513

commit v6 on v5

--- a/solution.py
+++ b/solution.py
@@ -235,36 +235,9 @@
             chosen = chosen | (t == step)
         pl.when(chosen)(action)
 
-    def kernel_step(t, carry):
-        late = t - 8
-        pair = jnp.where(t < 3, 0, jnp.where(t < 6, 1, jnp.where(t < 8, t - 6, pick(late // 4, (3, 2, 4)))))
-        ap = jnp.where(t < 6, pick(t % 3, (0, 1, 3)), jnp.where(t < 8, 2, late % 4))
-
-        def relay_first(a):
-            gather_first(a).wait_recv()
-            forward(a + 1).start()
-
-        once(t, (0,), lambda: turn((0, 1), (2, 3, 7, 8)))
-        once(t, (3,), lambda: turn((2, 3, 7, 8), (4, 5, 9)))
-        once(t, (12,), lambda: turn((4, 5), ()))
-        once(t, (16,), lambda: turn((9,), ()))
-        once(t, (0,), lambda: relay_first(2))
-        once(t, (1,), lambda: relay_first(6))
-        once(t, (4,), lambda: relay_first(4))
-
-        def new_second():
-            take_second(2 * pair)
-            take_second(2 * pair + 1)
-
-        def new_first():
-            gather_first(2 * ap + 1).wait_recv()
-            take_first(2 * ap)
-            take_first(2 * ap + 1)
-
-        once(t, (0, 3, 8, 12, 16), new_second)
-        once(t, (0, 1, 2, 6), new_first)
+    def form(pair, place, count):
         wide = lanes(pair, 2)
-        here = lanes(ap, 2)
+        here = lanes(place, 2 * count)
         product = matmul(za[here, :], bt[:, wide])
         value = jnp.exp2(product * scale)
         km[here, wide] = value.astype(BF16)
@@ -272,21 +245,57 @@
         across = (tiles[0] - tiles[2]) + (tiles[3] - tiles[5]) + (tiles[1] + tiles[4]) * tile_sign
         acc_a[here, :] += across
         parts = [
-            jnp.sum(value[each * j : each * (j + 1)].reshape(each // 8, 8, 2 * both), axis=0) for j in range(4)
+            jnp.sum(value[each * j : each * (j + 1)].reshape(each // 8, 8, 2 * both), axis=0) for j in range(4 * count)
         ]
-        acc_b[:, lanes(jnp.minimum(pair, TWO_SIDED), 2)] += (parts[0] - parts[1]) + (parts[2] - parts[3])
-
-        def second_done():
-            for b in (2 * pair, 2 * pair + 1):
-                here = block_lanes(b)
-                total = jnp.sum(acc_b[:, here], axis=0, keepdims=True) * sign
-                part_b[:, here] = total
-                partial_second(b).start()
-
-        once(t, (6, 7, 15), second_done)
-        return carry
-
-    lax.fori_loop(0, 4 * SECOND_PAIRS, kernel_step, 0)
+        down = sum(parts[2::2], parts[0]) - sum(parts[3::2], parts[1])
+        acc_b[:, lanes(jnp.minimum(pair, TWO_SIDED), 2)] += down
+
+    def new_second(pair):
+        take_second(2 * pair)
+        take_second(2 * pair + 1)
+
+    def second_done(pair):
+        for b in (2 * pair, 2 * pair + 1):
+            here = block_lanes(b)
+            part_b[:, here] = jnp.sum(acc_b[:, here], axis=0, keepdims=True) * sign
+            partial_second(b).start()
+
+    def early_step(t, carry):
+        pair = jnp.where(t < 6, t // 3, t - 6)
+        ap = jnp.where(t < 6, pick(t % 3, (0, 1, 3)), 2)
+
+        def relay_first(a):
+            gather_first(a).wait_recv()
+            forward(a + 1).start()
+
+        once(t, (0,), lambda: turn((0, 1), (2, 3, 7, 8)))
+        once(t, (3,), lambda: turn((2, 3, 7, 8), (4, 5, 9)))
+        once(t, (0,), lambda: relay_first(2))
+        once(t, (1,), lambda: relay_first(6))
+        once(t, (4,), lambda: relay_first(4))
+
+        def new_first():
+            gather_first(2 * ap + 1).wait_recv()
+            take_first(2 * ap)
+            take_first(2 * ap + 1)
+
+        once(t, (0, 3), lambda: new_second(pair))
+        once(t, (0, 1, 2, 6), new_first)
+        form(pair, ap, 1)
+        once(t, (6, 7), lambda: second_done(pair))
+        return carry
+
+    def late_step(t, carry):
+        pair = pick(t // 2, (3, 2, 4))
+        once(t, (2,), lambda: turn((4, 5), ()))
+        once(t, (4,), lambda: turn((9,), ()))
+        once(t, (0, 2, 4), lambda: new_second(pair))
+        form(pair, t % 2, 2)
+        once(t, (3,), lambda: second_done(pair))
+        return carry
+
+    lax.fori_loop(0, 8, early_step, 0)
+    lax.fori_loop(0, 6, late_step, 0)
 
     rows8 = none8
     for a in range(na):

time: 56.8 us -> 54.9 us (0.967)
  Pallas kernels: 56 us -> 54 us
    pallas_call x1, Pallas kernels: 54.3 us -> 52.4 us  [shards(): pl.pallas_call(kernel, out_shape=(jax.ShapeDtypeStruct((each, width), F32...]
where the time goes in v6:
time: 54.9 us; the launch traced here: 54.7 us
  Pallas kernels  54 us (98%)
  between operations  0.64 us (1%)
    pallas_call x1, Pallas kernels, shards(): pl.pallas_call(kernel, out_shape=(jax.ShapeDtypeStruct((each, width), F32...  52.4 us
    pallas_call x1, Pallas kernels, shards(): pl.pallas_call(hand_on, out_shape=(jax.ShapeDtypeStruct((each, width), F3...  1.63 us

profile of v6, /device:TPU:1, one launch (start us, length us, event | category | flops | bytes accessed | tf_op | source)
XLA Modules:
  0.0 54.7 jit_solution(7593298157524587307)
XLA Ops:
  0.6 52.4 %shard_map.49 = (f32[192,128]{1,0:T(8,128)}, f32[192,128]{1,0:T(8,128)}, f32[8,128]{1,0:T(8,128)}) custom-call(bf16[192,128]{1,0:T(8,128)(2,1)} %pool_ref.1, bf16[192,128]{1,0:T(8,128)(2,1)} %label_ref.1), custom_call_target="tpu_custom_call" | custom-call | tf_op jit(solution)/shard_map/pallas_call | solution.py:502
  53.0 1.6 %shard_map.50 = (f32[192,128]{1,0:T(8,128)}, f32[192,128]{1,0:T(8,128)}, f32[1,1]{1,0:T(1,128)}) custom-call(f32[192,128]{1,0:T(8,128)} %get-tuple-element.9.pool_in, f32[192,128]{1,0:T(8,128)} %get-tuple-element.10.label_in, f32[8,128]{1,0:T(8,128)} %get-tuple-element.11.objective_in), custom_call_target="tpu_custom_call" | custom-call | tf_op jit(solution)/shard_map/pallas_call | solution.py:522

commit v7 on v6

--- a/solution.py
+++ b/solution.py
@@ -286,16 +286,16 @@
         return carry
 
     def late_step(t, carry):
-        pair = pick(t // 2, (3, 2, 4))
-        once(t, (2,), lambda: turn((4, 5), ()))
-        once(t, (4,), lambda: turn((9,), ()))
-        once(t, (0, 2, 4), lambda: new_second(pair))
-        form(pair, t % 2, 2)
-        once(t, (3,), lambda: second_done(pair))
+        pair = pick(t, (3, 2, 4))
+        once(t, (1,), lambda: turn((4, 5), ()))
+        once(t, (2,), lambda: turn((9,), ()))
+        new_second(pair)
+        form(pair, 0, 4)
+        once(t, (1,), lambda: second_done(pair))
         return carry
 
     lax.fori_loop(0, 8, early_step, 0)
-    lax.fori_loop(0, 6, late_step, 0)
+    lax.fori_loop(0, 3, late_step, 0)
 
     rows8 = none8
     for a in range(na):

time: 54.9 us -> 54.5 us (level)
  no operation moved by 1% of the time
where the time goes in v7:
time: 54.5 us; the launch traced here: 54.3 us
  Pallas kernels  53.6 us (98%)
  between operations  0.64 us (1%)
    pallas_call x1, Pallas kernels, shards(): pl.pallas_call(kernel, out_shape=(jax.ShapeDtypeStruct((each, width), F32...  52 us
    pallas_call x1, Pallas kernels, shards(): pl.pallas_call(hand_on, out_shape=(jax.ShapeDtypeStruct((each, width), F3...  1.63 us

profile of v7, /device:TPU:1, one launch (start us, length us, event | category | flops | bytes accessed | tf_op | source)
XLA Modules:
  0.0 54.3 jit_solution(1750635585292989329)
XLA Ops:
  0.6 52.0 %shard_map.49 = (f32[192,128]{1,0:T(8,128)}, f32[192,128]{1,0:T(8,128)}, f32[8,128]{1,0:T(8,128)}) custom-call(bf16[192,128]{1,0:T(8,128)(2,1)} %pool_ref.1, bf16[192,128]{1,0:T(8,128)(2,1)} %label_ref.1), custom_call_target="tpu_custom_call" | custom-call | tf_op jit(solution)/shard_map/pallas_call | solution.py:502
  52.6 1.6 %shard_map.50 = (f32[192,128]{1,0:T(8,128)}, f32[192,128]{1,0:T(8,128)}, f32[1,1]{1,0:T(1,128)}) custom-call(f32[192,128]{1,0:T(8,128)} %get-tuple-element.9.pool_in, f32[192,128]{1,0:T(8,128)} %get-tuple-element.10.label_in, f32[8,128]{1,0:T(8,128)} %get-tuple-element.11.objective_in), custom_call_target="tpu_custom_call" | custom-call | tf_op jit(solution)/shard_map/pallas_call | solution.py:522

commit v8 on v7

--- a/solution.py
+++ b/solution.py
@@ -261,8 +261,7 @@
             partial_second(b).start()
 
     def early_step(t, carry):
-        pair = jnp.where(t < 6, t // 3, t - 6)
-        ap = jnp.where(t < 6, pick(t % 3, (0, 1, 3)), 2)
+        ap = pick(t, (0, 1, 3, 2))
 
         def relay_first(a):
             gather_first(a).wait_recv()
@@ -272,30 +271,30 @@
         once(t, (3,), lambda: turn((2, 3, 7, 8), (4, 5, 9)))
         once(t, (0,), lambda: relay_first(2))
         once(t, (1,), lambda: relay_first(6))
-        once(t, (4,), lambda: relay_first(4))
+        once(t, (2,), lambda: relay_first(4))
 
         def new_first():
             gather_first(2 * ap + 1).wait_recv()
             take_first(2 * ap)
             take_first(2 * ap + 1)
 
-        once(t, (0, 3), lambda: new_second(pair))
-        once(t, (0, 1, 2, 6), new_first)
-        form(pair, ap, 1)
-        once(t, (6, 7), lambda: second_done(pair))
+        once(t, (0,), lambda: new_second(0))
+        new_first()
+        form(0, ap, 1)
+        once(t, (3,), lambda: second_done(0))
         return carry
 
     def late_step(t, carry):
-        pair = pick(t, (3, 2, 4))
-        once(t, (1,), lambda: turn((4, 5), ()))
-        once(t, (2,), lambda: turn((9,), ()))
+        pair = pick(t, (1, 3, 2, 4))
+        once(t, (2,), lambda: turn((4, 5), ()))
+        once(t, (3,), lambda: turn((9,), ()))
         new_second(pair)
         form(pair, 0, 4)
-        once(t, (1,), lambda: second_done(pair))
-        return carry
-
-    lax.fori_loop(0, 8, early_step, 0)
-    lax.fori_loop(0, 3, late_step, 0)
+        once(t, (0, 2), lambda: second_done(pair))
+        return carry
+
+    lax.fori_loop(0, 4, early_step, 0)
+    lax.fori_loop(0, 4, late_step, 0)
 
     rows8 = none8
     for a in range(na):

time: 54.5 us -> 54.2 us (level)
  no operation moved by 1% of the time
where the time goes in v8:
time: 54.2 us; the launch traced here: 54 us
  Pallas kernels  53.4 us (99%)
  between operations  0.64 us (1%)
    pallas_call x1, Pallas kernels, shards(): pl.pallas_call(kernel, out_shape=(jax.ShapeDtypeStruct((each, width), F32...  51.8 us
    pallas_call x1, Pallas kernels, shards(): pl.pallas_call(hand_on, out_shape=(jax.ShapeDtypeStruct((each, width), F3...  1.63 us

profile of v8, /device:TPU:1, one launch (start us, length us, event | category | flops | bytes accessed | tf_op | source)
XLA Modules:
  0.0 54.0 jit_solution(5078776158071411766)
XLA Ops:
  0.6 51.8 %shard_map.49 = (f32[192,128]{1,0:T(8,128)}, f32[192,128]{1,0:T(8,128)}, f32[8,128]{1,0:T(8,128)}) custom-call(bf16[192,128]{1,0:T(8,128)(2,1)} %pool_ref.1, bf16[192,128]{1,0:T(8,128)(2,1)} %label_ref.1), custom_call_target="tpu_custom_call" | custom-call | tf_op jit(solution)/shard_map/pallas_call | solution.py:501
  52.4 1.6 %shard_map.50 = (f32[192,128]{1,0:T(8,128)}, f32[192,128]{1,0:T(8,128)}, f32[1,1]{1,0:T(1,128)}) custom-call(f32[192,128]{1,0:T(8,128)} %get-tuple-element.9.pool_in, f32[192,128]{1,0:T(8,128)} %get-tuple-element.10.label_in, f32[8,128]{1,0:T(8,128)} %get-tuple-element.11.objective_in), custom_call_target="tpu_custom_call" | custom-call | tf_op jit(solution)/shard_map/pallas_call | solution.py:521
